TPU v7x, 32 devices: a whole 2x2x4 slice. The times are simulated.
32 devices in a mesh: lat: 4 (over y, x), lon: 8 (over z, core).
Axes of the slice: x: 2, y: 2, z: 4, core: 2. Of those that a mesh axis runs over, the one named last changes fastest.
Arguments:
- states: bfloat16 [2, 144, 384, 192], P(None, 'lat', 'lon'), may hold values from -6 to 6
- cotangent: bfloat16 [2, 144, 384, 192], P(None, 'lat', 'lon'), may hold values from -9 to 9
- land_mask: int32 [144, 384], P('lat', 'lon'), may hold values 0 or 1
- pole_mask: int32 [144], P('lat'), may hold values from 0 to 1, as said below
- bias_table: float32 [12, 11, 3456], P('lat'), may hold values from -4 to 410
- norm_gain: float32 [192], replicated, may hold values from 0.5 to 1.5
- norm_shift: float32 [192], replicated, may hold values from -3 to 3
- in_weight: bfloat16 [192, 576], replicated, may hold values from -0.4375 to 0.4375
- in_bias: float32 [576], replicated, may hold values from -3 to 3
- out_weight: bfloat16 [192, 192], replicated, may hold values from -0.4375 to 0.4375
- land_gain: float32 [6], replicated, may hold values from -2 to 2
Outputs:
- grad_states: bfloat16 [2, 144, 384, 192], P(None, 'lat', 'lon')
- grad_in_weight: float32 [192, 576], replicated
- grad_in_bias: float32 [576], replicated
- grad_out_weight: float32 [192, 192], replicated
- grad_out_bias: float32 [192], replicated
- grad_norm_gain: float32 [192], replicated
- grad_norm_shift: float32 [192], replicated
- grad_land_gain: float32 [6], replicated
- grad_bias_table: float32 [12, 11, 3456], P('lat')
Inputs may be any that keep to these rules, and one draw needn't show every extreme that they name: `pole_mask`: pole padding: zero on the last P rows of the grid and one on all others, for some P from 1 to 5.
All inputs are finite; a program needn't handle non-finite values. No bound on the sum of `land_mask` on one device may be relied on, other than what follows from the above.
Results may differ from a plain program's by a relative error of at most 0.0095.
Values may be sent and summed in bfloat16 or wider, within the bound.
A program may use at most 128 MiB of HBM per device.

v0:
```python
import jax
import jax.numpy as jnp
from jax import lax
from jax.sharding import PartitionSpec as P

C = 192
HEADS = 6
PL = 2
WLAT = 12
WLON = 6
S_LAT = 6
S_LON = 3
WT = 144
DL = 11
NPOS = 3456


EPSILON = 1e-05
TARGET_RMS = 0.5
RMS_EPSILON = 1e-06


def as_sent(array):

    def short(part):
        return part.astype(jnp.bfloat16) if part.dtype == jnp.float32 else part

    return jax.tree.map(short, array)


def passed_along(array, axis, by):
    size = lax.axis_size(axis)
    return lax.ppermute(array, axis, [(i, (i + by) % size) for i in range(size)])


def lon_onehot():
    offsets = jnp.arange(DL, dtype=jnp.int32)[:, None, None]
    query_col = jnp.arange(WLON, dtype=jnp.int32)[None, :, None]
    key_col = jnp.arange(WLON, dtype=jnp.int32)[None, None, :]
    return (query_col - key_col + WLON - 1 == offsets).astype(jnp.float32)


def expand_bias(table_row):
    shaped = table_row.reshape(DL, HEADS, PL, PL, WLAT, WLAT)
    full_bias = jnp.einsum(
        "dhabij,dxy->haixbjy", shaped, lon_onehot(), precision=lax.Precision.HIGHEST
    )
    return full_bias.reshape(HEADS, WT, WT)


def collapse_bias(grad_full):
    shaped = grad_full.reshape(HEADS, PL, WLAT, WLON, PL, WLAT, WLON)
    folded = jnp.einsum(
        "haixbjy,dxy->dhabij", shaped, lon_onehot(), precision=lax.Precision.HIGHEST
    )
    return folded.reshape(DL, NPOS)


def allowed_pairs(row_part, row_valid):
    part_tok = jnp.tile(jnp.repeat(row_part, WLON), PL)
    valid_tok = jnp.tile(jnp.repeat(row_valid, WLON), PL)
    return (part_tok[:, None] == part_tok[None, :]) & (valid_tok[None, :] > 0)


def band_windows(grid):
    row_count = grid.shape[1]
    col_count = grid.shape[2]
    feat_count = grid.shape[3]
    split = grid.reshape(PL, row_count // WLAT, WLAT, col_count // WLON, WLON, feat_count)
    return split.transpose(1, 3, 0, 2, 4, 5).reshape(
        row_count // WLAT, col_count // WLON, WT, feat_count
    )


def window_block(
    tokens,
    cot_win,
    land_tok,
    allowed,
    table_row,
    norm_gain,
    norm_shift,
    in_weight,
    in_bias,
    out_weight,
    land_gain,
):
    f32 = jnp.float32
    head_dim = C // HEADS
    qk_scale = head_dim ** (-0.5)
    weight_heads = in_weight.reshape(C, 3, HEADS, head_dim)
    out_heads = out_weight.reshape(HEADS, head_dim, C)
    floats = tokens.astype(f32)
    center = floats - jnp.mean(floats, axis=-1, keepdims=True)
    inv_std = lax.rsqrt(jnp.mean(center * center, axis=-1, keepdims=True) + EPSILON)
    normed = center * inv_std
    hidden = (normed * norm_gain + norm_shift).astype(jnp.bfloat16)
    projected = jnp.einsum("wtc,cghd->gwhtd", hidden, weight_heads, preferred_element_type=f32)
    projected = projected + in_bias.reshape(3, HEADS, head_dim)[:, None, :, None, :]
    packed = projected.astype(jnp.bfloat16)
    queries = packed[0]
    key_rows = packed[1]
    value_rows = packed[2]
    scores = jnp.einsum("whqd,whkd->whqk", queries, key_rows, preferred_element_type=f32) * qk_scale
    scores = (
        scores
        + expand_bias(table_row)[None]
        + land_gain[None, :, None, None] * land_tok[:, None, None, :]
    )
    pair_gate = allowed[None, None]
    row_top = jnp.max(jnp.where(pair_gate, scores, -jnp.inf), axis=-1, keepdims=True)
    exp_terms = jnp.where(pair_gate, jnp.exp(scores - row_top), 0.0)
    probs = exp_terms / jnp.sum(exp_terms, axis=-1, keepdims=True)
    probs_low = probs.astype(jnp.bfloat16)
    mixed_out = jnp.einsum("whqk,whkd->whqd", probs_low, value_rows, preferred_element_type=f32)
    mixed_low = mixed_out.astype(jnp.bfloat16)
    grad_out_weight = jnp.einsum(
        "whqd,wqo->hdo", mixed_low, cot_win, preferred_element_type=f32
    ).reshape(C, C)
    grad_out_bias = jnp.sum(cot_win.astype(f32), axis=(0, 1))
    grad_mixed = jnp.einsum("wqo,hdo->whqd", cot_win, out_heads, preferred_element_type=f32).astype(
        jnp.bfloat16
    )
    grad_probs = jnp.einsum("whqd,whkd->whqk", grad_mixed, value_rows, preferred_element_type=f32)
    grad_values = jnp.einsum("whqk,whqd->whkd", probs_low, grad_mixed, preferred_element_type=f32)
    grad_scores = probs * (grad_probs - jnp.sum(grad_probs * probs, axis=-1, keepdims=True))
    grad_land = jnp.einsum("whqk,wk->h", grad_scores, land_tok, precision=lax.Precision.HIGHEST)
    grad_table = collapse_bias(jnp.sum(grad_scores, axis=0))
    scores_low = grad_scores.astype(jnp.bfloat16)
    grad_queries = (
        jnp.einsum("whqk,whkd->whqd", scores_low, key_rows, preferred_element_type=f32) * qk_scale
    )
    grad_keys = (
        jnp.einsum("whqk,whqd->whkd", scores_low, queries, preferred_element_type=f32) * qk_scale
    )
    grad_packed = jnp.stack([grad_queries, grad_keys, grad_values], axis=0)
    grad_in_bias = jnp.sum(grad_packed, axis=(1, 3)).reshape(3 * C)
    packed_low = grad_packed.astype(jnp.bfloat16)
    grad_in_weight = jnp.einsum(
        "wtc,gwhtd->cghd", hidden, packed_low, preferred_element_type=f32
    ).reshape(C, 3 * C)
    grad_hidden = jnp.einsum(
        "gwhtd,cghd->wtc", packed_low, weight_heads, preferred_element_type=f32
    )
    grad_gain = jnp.sum(grad_hidden * normed, axis=(0, 1))
    grad_shift = jnp.sum(grad_hidden, axis=(0, 1))
    scaled = grad_hidden * norm_gain
    grad_tokens = inv_std * (
        scaled
        - jnp.mean(scaled, axis=-1, keepdims=True)
        - normed * jnp.mean(scaled * normed, axis=-1, keepdims=True)
    )
    dense_terms = (
        grad_in_weight,
        grad_in_bias,
        grad_out_weight,
        grad_out_bias,
        grad_gain,
        grad_shift,
        grad_land,
    )
    return (grad_tokens.astype(jnp.bfloat16), dense_terms, grad_table)


def lon_rim(pieces, offset):
    return jax.tree.map(
        lambda part, own: part.astype(own.dtype),
        passed_along(as_sent(pieces), "lon", offset),
        pieces,
    )


def lat_rim(pieces, offset):
    return jax.tree.map(
        lambda part, own: part.astype(own.dtype),
        passed_along(as_sent(pieces), "lat", offset),
        pieces,
    )


def normalize_rms(gradient):
    rms_value = jnp.sqrt(jnp.mean(gradient * gradient) + RMS_EPSILON)
    return gradient * (TARGET_RMS / rms_value)


def local(
    states,
    cotangent,
    land_mask,
    pole_mask,
    bias_table,
    norm_gain,
    norm_shift,
    in_weight,
    in_bias,
    out_weight,
    land_gain,
):
    lat_rows = states.shape[1]
    col_count = states.shape[2]
    band_count = lat_rows // WLAT
    land_low = land_mask.astype(jnp.bfloat16)
    pole_low = pole_mask.astype(jnp.bfloat16)
    ahead_rim = lon_rim((states[:, :, :S_LON], cotangent[:, :, :S_LON], land_low[:, :S_LON]), -1)
    states_one = jnp.concatenate([states[:, :, S_LON:], ahead_rim[0]], axis=2)
    cot_one = jnp.concatenate([cotangent[:, :, S_LON:], ahead_rim[1]], axis=2)
    land_one = jnp.concatenate([land_low[:, S_LON:], ahead_rim[2]], axis=1)
    above_rim = lat_rim(
        (states_one[:, :S_LAT], cot_one[:, :S_LAT], land_one[:S_LAT], pole_low[:S_LAT]), -1
    )
    rolled = jnp.concatenate([states_one[:, S_LAT:], above_rim[0]], axis=1)
    rolled_cot = jnp.concatenate([cot_one[:, S_LAT:], above_rim[1]], axis=1)
    rolled_land = jnp.concatenate([land_one[S_LAT:], above_rim[2]], axis=0).astype(jnp.float32)
    rolled_pole = jnp.concatenate([pole_low[S_LAT:], above_rim[3]], axis=0)
    total_rows = lat_rows * lax.axis_size("lat")
    row_ids = lax.axis_index("lat") * lat_rows + jnp.arange(lat_rows, dtype=jnp.int32)
    row_part = (row_ids >= total_rows - S_LAT).astype(jnp.int32).reshape(band_count, WLAT)
    pole_valid = (rolled_pole > 0.5).astype(jnp.int32).reshape(band_count, WLAT)
    tokens_all = band_windows(rolled)
    cot_all = band_windows(rolled_cot)
    land_all = band_windows(
        jnp.broadcast_to(rolled_land[None, :, :, None], (PL, lat_rows, col_count, 1))
    )[..., 0]

    def one_band(band_items):
        tokens, cot_win, land_tok, part_row, valid_row, table_row = band_items
        pairs = allowed_pairs(part_row, valid_row)
        return window_block(
            tokens,
            cot_win,
            land_tok,
            pairs,
            table_row,
            norm_gain,
            norm_shift,
            in_weight,
            in_bias,
            out_weight,
            land_gain,
        )

    grad_win, dense_rows, local_table = lax.map(
        one_band, (tokens_all, cot_all, land_all, row_part, pole_valid, bias_table)
    )
    grad_grid = (
        grad_win.reshape(band_count, col_count // WLON, PL, WLAT, WLON, C)
        .transpose(2, 0, 3, 1, 4, 5)
        .reshape(PL, lat_rows, col_count, C)
    )
    below_rim = lat_rim((grad_grid[:, lat_rows - S_LAT :],), 1)
    grad_lat = jnp.concatenate([below_rim[0], grad_grid[:, : lat_rows - S_LAT]], axis=1)
    behind = lon_rim((grad_lat[:, :, col_count - S_LON :],), 1)
    grad_back = jnp.concatenate([behind[0], grad_lat[:, :, : col_count - S_LON]], axis=2)
    grad_states = (cotangent.astype(jnp.float32) + grad_back.astype(jnp.float32)).astype(
        jnp.bfloat16
    )
    in_w_part = jnp.sum(dense_rows[0], axis=0)
    in_b_part = jnp.sum(dense_rows[1], axis=0)
    out_w_part = jnp.sum(dense_rows[2], axis=0)
    out_b_part = jnp.sum(dense_rows[3], axis=0)
    gain_part = jnp.sum(dense_rows[4], axis=0)
    shift_part = jnp.sum(dense_rows[5], axis=0)
    land_part = jnp.sum(dense_rows[6], axis=0)
    dense_sums = lax.psum(
        (in_w_part, in_b_part, out_w_part, out_b_part, gain_part, shift_part, land_part),
        ("lat", "lon"),
    )
    table_sum = lax.psum(local_table, "lon")
    table_sq = lax.psum(jnp.sum(table_sum * table_sum), "lat")
    table_count = band_count * lax.axis_size("lat") * DL * NPOS
    table_rms = jnp.sqrt(table_sq / table_count + RMS_EPSILON)
    grad_bias_table = table_sum * (TARGET_RMS / table_rms)
    return (
        grad_states,
        normalize_rms(dense_sums[0]),
        normalize_rms(dense_sums[1]),
        normalize_rms(dense_sums[2]),
        normalize_rms(dense_sums[3]),
        normalize_rms(dense_sums[4]),
        normalize_rms(dense_sums[5]),
        normalize_rms(dense_sums[6]),
        grad_bias_table,
    )


def solution(mesh):
    return jax.shard_map(
        local,
        mesh=mesh,
        in_specs=(
            P(None, "lat", "lon", None),
            P(None, "lat", "lon", None),
            P("lat", "lon"),
            P("lat"),
            P("lat", None, None),
            P(),
            P(),
            P(),
            P(),
            P(),
            P(),
        ),
        out_specs=(
            P(None, "lat", "lon", None),
            P(),
            P(),
            P(),
            P(),
            P(),
            P(),
            P(),
            P("lat", None, None),
        ),
        check_vma=False,
    )
```

profile of v0, /device:TPU:1, one launch (start us, length us, event | category | flops | bytes accessed | tf_op | source)
XLA Modules:
  0.0 844.2 jit_solution(7171446748395053910)
XLA Ops:
  56.2 572.7 %while.30 = (s32[]{:T(128)}, bf16[3,8,144,192]{3,1,2,0:T(8,128)(2,1)}, f32[3,192,576]{2,1,0:T(8,128)}, f32[3,576]{1,0:T(4,128)}, f32[3,192,192]{2,1,0:T(8,128)},...) while((s32[]{:T(128)}, ...), condition=%wide.region_14.15_spmd, body=%wide.region_0.14_spmd.sunk | while | flops 1451403776 | bytes 133005200 | solution.py:242
  101.7 19.8 %copy.204 = f32[6,2,12,6,2,12,6]{3,2,1,6,5,4,0:T(8,128)} copy(f32[6,2,12,6,2,12,6]{5,6,2,4,1,0,3:T(8,128)} %convolution_bitcast_fusion.8) | data formatting | bytes 995328 | tf_op jit(solution)/shard_map/while/body/eval_jaxpr/add | solution.py:106
  121.5 11.8 %reshape.328 = f32[6,144,144]{1,2,0:T(8,128)} reshape(f32[6,2,12,6,2,12,6]{3,2,1,6,5,4,0:T(8,128)} %copy.204) | data formatting | bytes 995328 | tf_op jit(solution)/shard_map/while/body/eval_jaxpr/add | solution.py:106
  133.3 8.2 fusion.175
  179.5 12.9 %reshape.329 = f32[6,2,12,6,2,12,6]{3,2,1,6,5,4,0:T(8,128)} reshape(f32[6,144,144]{1,2,0:T(8,128)S(1)} %copy-done.9) | data formatting | bytes 995328 | tf_op jit(solution)/shard_map/while/body/eval_jaxpr/reshape | solution.py:52
  192.3 34.5 %copy.206 = f32[6,2,12,6,2,12,6]{6,5,3,4,2,1,0:T(8,128)} copy(f32[6,2,12,6,2,12,6]{3,2,1,6,5,4,0:T(8,128)} %reshape.329) | data formatting | bytes 995328 | tf_op jit(solution)/shard_map/while/body/eval_jaxpr/reshape | solution.py:52
  226.9 27.8 %convolution_bitcast_fusion.10 = f32[11,6,2,2,12,12]{5,0,3,4,2,1:T(8,128)S(1)} fusion(f32[6,2,12,6,2,12,6]{6,5,3,4,2,1,0:T(8,128)} %copy.206, s32[6,6]{1,0:T(8,128)S(1)} %subtract_add_fusion.2), kind=kOutput, calls=%fused_computation.34.clone.1 | convolution fusion | flops 16423704 | bytes 649872 | tf_op jit(solution)/shard_map/while/body/eval_jaxpr/haixbjy,dxy->dhabij/dot_general | solution.py:53
  276.2 6.8 convolution_bitcast_fusion.8
  283.0 19.8 %copy.204 = f32[6,2,12,6,2,12,6]{3,2,1,6,5,4,0:T(8,128)} copy(f32[6,2,12,6,2,12,6]{5,6,2,4,1,0,3:T(8,128)} %convolution_bitcast_fusion.8) | data formatting | bytes 995328 | tf_op jit(solution)/shard_map/while/body/eval_jaxpr/add | solution.py:106
  302.7 11.8 %reshape.328 = f32[6,144,144]{1,2,0:T(8,128)} reshape(f32[6,2,12,6,2,12,6]{3,2,1,6,5,4,0:T(8,128)} %copy.204) | data formatting | bytes 995328 | tf_op jit(solution)/shard_map/while/body/eval_jaxpr/add | solution.py:106
  314.5 8.2 fusion.175
  360.7 12.9 %reshape.329 = f32[6,2,12,6,2,12,6]{3,2,1,6,5,4,0:T(8,128)} reshape(f32[6,144,144]{1,2,0:T(8,128)S(1)} %copy-done.9) | data formatting | bytes 995328 | tf_op jit(solution)/shard_map/while/body/eval_jaxpr/reshape | solution.py:52
  373.6 34.5 %copy.206 = f32[6,2,12,6,2,12,6]{6,5,3,4,2,1,0:T(8,128)} copy(f32[6,2,12,6,2,12,6]{3,2,1,6,5,4,0:T(8,128)} %reshape.329) | data formatting | bytes 995328 | tf_op jit(solution)/shard_map/while/body/eval_jaxpr/reshape | solution.py:52
  408.1 27.8 %convolution_bitcast_fusion.10 = f32[11,6,2,2,12,12]{5,0,3,4,2,1:T(8,128)S(1)} fusion(f32[6,2,12,6,2,12,6]{6,5,3,4,2,1,0:T(8,128)} %copy.206, s32[6,6]{1,0:T(8,128)S(1)} %subtract_add_fusion.2), kind=kOutput, calls=%fused_computation.34.clone.1 | convolution fusion | flops 16423704 | bytes 649872 | tf_op jit(solution)/shard_map/while/body/eval_jaxpr/haixbjy,dxy->dhabij/dot_general | solution.py:53
  464.2 19.8 %copy.204 = f32[6,2,12,6,2,12,6]{3,2,1,6,5,4,0:T(8,128)} copy(f32[6,2,12,6,2,12,6]{5,6,2,4,1,0,3:T(8,128)} %convolution_bitcast_fusion.8) | data formatting | bytes 995328 | tf_op jit(solution)/shard_map/while/body/eval_jaxpr/add | solution.py:106
  484.0 11.8 %reshape.328 = f32[6,144,144]{1,2,0:T(8,128)} reshape(f32[6,2,12,6,2,12,6]{3,2,1,6,5,4,0:T(8,128)} %copy.204) | data formatting | bytes 995328 | tf_op jit(solution)/shard_map/while/body/eval_jaxpr/add | solution.py:106
  495.7 8.2 fusion.175
  542.0 12.9 %reshape.329 = f32[6,2,12,6,2,12,6]{3,2,1,6,5,4,0:T(8,128)} reshape(f32[6,144,144]{1,2,0:T(8,128)S(1)} %copy-done.9) | data formatting | bytes 995328 | tf_op jit(solution)/shard_map/while/body/eval_jaxpr/reshape | solution.py:52
  554.8 34.5 %copy.206 = f32[6,2,12,6,2,12,6]{6,5,3,4,2,1,0:T(8,128)} copy(f32[6,2,12,6,2,12,6]{3,2,1,6,5,4,0:T(8,128)} %reshape.329) | data formatting | bytes 995328 | tf_op jit(solution)/shard_map/while/body/eval_jaxpr/reshape | solution.py:52
  589.4 27.8 %convolution_bitcast_fusion.10 = f32[11,6,2,2,12,12]{5,0,3,4,2,1:T(8,128)S(1)} fusion(f32[6,2,12,6,2,12,6]{6,5,3,4,2,1,0:T(8,128)} %copy.206, s32[6,6]{1,0:T(8,128)S(1)} %subtract_add_fusion.2), kind=kOutput, calls=%fused_computation.34.clone.1 | convolution fusion | flops 16423704 | bytes 649872 | tf_op jit(solution)/shard_map/while/body/eval_jaxpr/haixbjy,dxy->dhabij/dot_general | solution.py:53
  631.8 39.2 %all-reduce = (f32[576]{0:T(1024)S(1)}, f32[192]{0:T(256)S(1)}, f32[192]{0:T(256)S(1)}, f32[192]{0:T(256)S(1)}, f32[6]{0:T(128)S(1)}) all-reduce(f32[576]{0:T(1024)S(1)} %reduce_sum.317, f32[192]{0:T(256)S(1)} %reduce_sum.321, f32[192]{0:T(256)S(1)} %reduce_sum.323, ...), channel_id=1, replica_groups=mesh['lat'=4,'lon'=8] {'lat','lon'}, use_global_device_ids=true, to_apply=%region_19.20 | all-reduce | flops 1158 | bytes 9264 | tf_op jit(solution)/shard_map/psum | solution.py:264
  687.3 7.0 collective-permute-done.7
  710.8 109.0 %all-reduce.7.cloned.1.call-done = (f32[192,576]{1,0:T(8,128)}, f32[192,192]{1,0:T(8,128)}) async-done(((f32[192,576]{1,0:T(8,128)}, f32[192,192]{1,0:T(8,128)}), (f32[192,576]{1,0:T(8,128)}, f32[192,192]{1,0:T(8,128)})) %all-reduce.7.cloned.1.call-update) | async-done | bytes 589840 | tf_op jit(solution)/shard_map/psum | solution.py:264
  828.0 7.7 add_convert_fusion.1
  (389 shorter events, 279.7 us)
Async XLA Ops:
  7.2 687.9 %all-reduce.5.cloned.1.call-start = ((), (), s32[]{:S(2)}) async-start(), calls=%async_computation | async-start | bytes 1216512 | tf_op jit(solution)/shard_map/psum | solution.py:268
  7.9 19.8 %collective-permute-start.2 = (bf16[6]{0:T(256)(128)(2,1)S(1)}, bf16[6]{0:T(256)(128)(2,1)}, u32[]{:S(2)}, u32[]{:S(2)}) collective-permute-start(bf16[6]{0:T(256)(128)(2,1)S(1)} %bitcast.315), channel_id=1, source_target_pairs={{0,24},{8,0},{16,8},{24,16},{1,25},{9,1},{17,9},{25,17},{2,26},{10... | collective-permute-start | bytes 44 | tf_op jit(solution)/shard_map/ppermute | solution.py:33
  12.2 16.9 %collective-permute-start.3 = (bf16[36,3]{1,0:T(8,128)(2,1)}, bf16[36,3]{1,0:T(8,128)(2,1)}, u32[]{:S(2)}, u32[]{:S(2)}) collective-permute-start(bf16[36,3]{1,0:T(8,128)(2,1)} %bitcast.198), channel_id=1, source_target_pairs={{0,7},{1,0},{2,1},{3,2},{4,3},{5,4},{6,5},{7,6},{8,15},{9,8},{10,9... | collective-permute-start | bytes 656 | tf_op jit(solution)/shard_map/ppermute | solution.py:33
  14.8 25.1 %collective-permute-start.5 = (bf16[2,36,3,192]{3,2,1,0:T(4,128)(2,1)}, bf16[2,36,3,192]{3,2,1,0:T(4,128)(2,1)}, u32[]{:S(2)}, u32[]{:S(2)}) collective-permute-start(bf16[2,36,3,192]{3,2,1,0:T(4,128)(2,1)} %slice.92), channel_id=1, source_target_pairs={{0,7},{1,0},{2,1},{3,2},{4,3},{5,4},{6,5},{7,6},{8,15},{9,8},{10,9... | collective-permute-start | bytes 248840 | tf_op jit(solution)/shard_map/ppermute | solution.py:33
  19.2 18.7 %collective-permute-start = (bf16[2,36,3,192]{3,2,1,0:T(4,128)(2,1)}, bf16[2,36,3,192]{3,2,1,0:T(4,128)(2,1)}, u32[]{:S(2)}, u32[]{:S(2)}) collective-permute-start(bf16[2,36,3,192]{3,2,1,0:T(4,128)(2,1)} %slice.82), channel_id=1, source_target_pairs={{0,7},{1,0},{2,1},{3,2},{4,3},{5,4},{6,5},{7,6},{8,15},{9,8},{10,9... | collective-permute-start | bytes 248840 | tf_op jit(solution)/shard_map/ppermute | solution.py:33
  29.9 2.4 collective-permute-start.4
  38.7 7.4 collective-permute-start.1
  40.7 11.7 %collective-permute-start.6 = (bf16[2,6,48,192]{3,2,1,0:T(8,128)(2,1)S(1)}, bf16[2,6,48,192]{3,2,1,0:T(8,128)(2,1)S(1)}, u32[]{:S(2)}, u32[]{:S(2)}) collective-permute-start(bf16[2,6,48,192]{3,2,1,0:T(8,128)(2,1)S(1)} %pad_maximum_fusion.4), channel_id=1, source_target_pairs={{0,24},{8,0},{16,8},{24,16},{1,25},{9,1},{17,9},{25,17},{2,26},{10... | collective-permute-start | bytes 663560 | tf_op jit(solution)/shard_map/ppermute | solution.py:33
  86.1 5.4 copy-start.4
  86.3 5.2 copy-start.27
  121.5 11.8 %copy-start.10 = (bf16[3,8,6,144,32]{3,4,2,0,1:T(8,128)(2,1)S(1)}, bf16[3,8,6,144,32]{3,4,2,0,1:T(8,128)(2,1)}, u32[]{:S(2)}) copy-start(bf16[3,8,6,144,32]{3,4,2,0,1:T(8,128)(2,1)} %fusion.174) | copy-start | bytes 3981316 | tf_op jit(solution)/shard_map/while
  141.4 7.9 copy-start.14
  267.3 5.4 copy-start.4
  267.6 5.2 copy-start.27
  302.7 11.8 %copy-start.10 = (bf16[3,8,6,144,32]{3,4,2,0,1:T(8,128)(2,1)S(1)}, bf16[3,8,6,144,32]{3,4,2,0,1:T(8,128)(2,1)}, u32[]{:S(2)}) copy-start(bf16[3,8,6,144,32]{3,4,2,0,1:T(8,128)(2,1)} %fusion.174) | copy-start | bytes 3981316 | tf_op jit(solution)/shard_map/while
  322.7 7.9 copy-start.14
  448.6 5.4 copy-start.4
  448.8 5.2 copy-start.27
  484.0 11.8 %copy-start.10 = (bf16[3,8,6,144,32]{3,4,2,0,1:T(8,128)(2,1)S(1)}, bf16[3,8,6,144,32]{3,4,2,0,1:T(8,128)(2,1)}, u32[]{:S(2)}) copy-start(bf16[3,8,6,144,32]{3,4,2,0,1:T(8,128)(2,1)} %fusion.174) | copy-start | bytes 3981316 | tf_op jit(solution)/shard_map/while
  503.9 7.9 copy-start.14
  628.9 190.9 %all-reduce.7.cloned.1.call-start = ((), (), s32[]{:S(2)}) async-start(), calls=%async_computation.1 | async-start | bytes 1376256 | tf_op jit(solution)/shard_map/psum | solution.py:264
  685.7 8.6 %collective-permute-start.7 = (bf16[2,6,48,192]{3,0,2,1:T(2,128)(2,1)S(1)}, bf16[2,6,48,192]{3,0,2,1:T(2,128)(2,1)S(1)}, u32[]{:S(2)}, u32[]{:S(2)}) collective-permute-start(bf16[2,6,48,192]{3,0,2,1:T(2,128)(2,1)S(1)} %copy-done.20), channel_id=1, source_target_pairs={{0,8},{8,16},{16,24},{24,0},{1,9},{9,17},{17,25},{25,1},{2,10},{10... | collective-permute-start | bytes 663560 | tf_op jit(solution)/shard_map/ppermute | solution.py:33
  697.1 130.9 %copy-start.13 = (bf16[2,36,48,192]{3,2,1,0:T(8,128)(2,1)S(1)}, bf16[2,36,48,192]{3,2,1,0:T(8,128)(2,1)}, u32[]{:S(2)}) copy-start(bf16[2,36,48,192]{3,2,1,0:T(8,128)(2,1)} %param.14) | copy-start | bytes 3981316
  697.1 130.9 %collective-permute-start.8 = (bf16[2,36,3,192]{3,0,2,1:T(2,128)(2,1)}, bf16[2,36,3,192]{3,0,2,1:T(2,128)(2,1)}, u32[]{:S(2)}, u32[]{:S(2)}) collective-permute-start(bf16[2,36,3,192]{3,0,2,1:T(2,128)(2,1)} %pad_maximum_fusion.6), channel_id=1, source_target_pairs={{0,1},{1,2},{2,3},{3,4},{4,5},{5,6},{6,7},{7,0},{8,9},{9,10},{10,1... | collective-permute-start | bytes 248840 | tf_op jit(solution)/shard_map/ppermute | solution.py:33
  (60 other events, 194.3 us)
Sparse Core Ops, SparseCore 0:
  629.0 54.6 all-reduce.4
  689.6 130.1 all-reduce.6
where the time goes:
time: 855 us; the launch traced here: 844 us
  local copies, waits for them, and re-layouts  337 us (39%)
  matrix products  209 us (24%)
  waiting for transfers between devices  123 us (14%)
  other arithmetic  65.3 us (8%)
  blocking collectives  46 us (5%)
  loops' own time  30 us (4%)
  between operations  20 us (2%)
  starting transfers between devices  14.2 us (2%)
    reshape x6, local copies, waits for them, and re-layouts, collapse_bias(): shaped = grad_full.reshape(HEADS, PL, WLAT, WLON, PL, WLAT, WLON)  142 us
    psum x1, waiting for transfers between devices, local(): lax.psum((in_w_part, in_b_part, out_w_part, out_b_part, gain_part, shift_...  109 us
    add x6, local copies, waits for them, and re-layouts, window_block(): scores + expand_bias(table_row)[None]  94.6 us
    dot_general x3, matrix products, collapse_bias(): jnp.einsum('haixbjy,dxy->dhabij', shaped, lon_onehot(), precision=lax.Pre...  83.5 us
    psum x1, blocking collectives, local(): lax.psum((in_w_part, in_b_part, out_w_part, out_b_part, gain_part, shift_...  39.2 us
    another operation x1, loops' own time, local(): lax.map(one_band, (tokens_all, cot_all, land_all, row_part, pole_valid, b...  30 us
    dynamic_update_slice x21, local copies, waits for them, and re-layouts, local(): lax.map(one_band, (tokens_all, cot_all, land_all, row_part, pole_valid, b...  29.9 us
    sub x3, matrix products, window_block(): exp_terms = jnp.where(pair_gate, jnp.exp(scores - row_top), 0.0)  24.6 us
  transfers between devices with their start and end apart: 11, of which 5 were waited for; matrix products, arithmetic and copies ran while one was open for 7% of the time, Pallas kernels for 0%

commit v1 on v0

v1 whole, which is shorter than its diff:
```python
import jax
import jax.numpy as jnp
from jax import lax
from jax.experimental import pallas as pl
from jax.experimental.pallas import tpu as pltpu
from jax.sharding import PartitionSpec as P

C = 192
HEADS = 6
HD = C // HEADS
PL = 2
WLAT = 12
WLON = 6
S_LAT = 6
S_LON = 3
WT = 144
DL = 11
NPOS = 3456
COL = PL * WLAT
HL = HEADS * WT
TL = DL * COL

EPSILON = 1e-05
TARGET_RMS = 0.5
RMS_EPSILON = 1e-06
FAR = -1e30
F32 = jnp.float32
BF16 = jnp.bfloat16


def moved(array, axes, sizes, by):
    if isinstance(axes, str):
        size = sizes[axes]
        return lax.ppermute(array, axes, [(i, (i + by) % size) for i in range(size)])
    lat, lon = sizes["lat"], sizes["lon"]
    pairs = [
        (a * lon + b, ((a + by) % lat) * lon + (b + by) % lon)
        for a in range(lat)
        for b in range(lon)
    ]
    return lax.ppermute(array, axes, pairs)


def dot(a, b):
    return jnp.dot(a, b, preferred_element_type=F32)


def dot_nt(a, b):
    return lax.dot_general(a, b, (((1,), (1,)), ((), ())), preferred_element_type=F32)


def by_head(rows, head_masks):
    return jnp.concatenate([rows * m for m in head_masks], axis=0)


def diagonal(full):
    return jnp.concatenate(
        [full[HD * h : HD * (h + 1), WT * h : WT * (h + 1)] for h in range(HEADS)], axis=0
    )


def kernel(
    windows,
    per_step,
    tok_ref,
    cot_ref,
    land_ref,
    table_ref,
    gain_ref,
    shift_ref,
    win_ref,
    win_t_ref,
    bin_ref,
    wout_t_ref,
    lg_ref,
    grad_ref,
    dwin_ref,
    dbin_ref,
    dwout_ref,
    dbout_ref,
    dgain_ref,
    dshift_ref,
    dland_ref,
    dtable_ref,
    bias_s,
    acc_s,
):
    band = pl.program_id(0)
    step = pl.program_id(1)
    scale = HD ** (-0.5)

    @pl.when((band == 0) & (step == 0))
    def _():
        for ref in (dwin_ref, dbin_ref, dwout_ref, dbout_ref, dgain_ref, dshift_ref, dland_ref):
            ref[...] = jnp.zeros_like(ref)

    @pl.when(step == 0)
    def _():
        acc_s[...] = jnp.zeros_like(acc_s)
        for h in range(HEADS):
            for j in range(WLON):
                start = h * TL + (WLON - 1 - j) * COL
                bias_s[j * COL : (j + 1) * COL, h * WT : (h + 1) * WT] = table_ref[
                    0, :, start : start + WT
                ]

    lane = lax.broadcasted_iota(jnp.int32, (1, C), 1) // HD
    head_masks = [(lane == h).astype(F32).astype(BF16) for h in range(HEADS)]
    land_lane = lax.broadcasted_iota(jnp.int32, (1, windows), 1)

    for k in range(per_step):
        tok = tok_ref[k].astype(F32)
        center = tok - jnp.mean(tok, axis=-1, keepdims=True)
        inv_std = lax.rsqrt(jnp.mean(center * center, axis=-1, keepdims=True) + EPSILON)
        normed = center * inv_std
        hidden_f = normed * gain_ref[...] + shift_ref[...]
        hidden = hidden_f.astype(BF16)
        packed = (dot(hidden, win_ref[...]) + bin_ref[...]).astype(BF16)
        queries = packed[:, :C]
        keys = packed[:, C : 2 * C]
        values = packed[:, 2 * C :]
        q_heads = by_head(queries, head_masks)
        land = jnp.sum(
            jnp.where(land_lane == step * per_step + k, land_ref[0], 0.0), axis=1, keepdims=True
        )
        scores = dot_nt(keys, q_heads) * scale + bias_s[...] + land * lg_ref[...]
        top = jnp.max(scores, axis=0, keepdims=True)
        expd = jnp.exp(scores - top)
        probs = expd * (1.0 / jnp.sum(expd, axis=0, keepdims=True))
        probs_low = probs.astype(BF16)
        mixed_t = diagonal(dot(values.astype(F32).T.astype(BF16), probs_low)).astype(BF16)
        cot = cot_ref[k]
        dwout_ref[...] += dot(mixed_t, cot)
        dbout_ref[...] += jnp.sum(cot.astype(F32), axis=0, keepdims=True)
        grad_mixed = dot(cot, wout_t_ref[...]).astype(BF16)
        m_heads = by_head(grad_mixed, head_masks)
        grad_probs = dot_nt(values, m_heads)
        grad_values = dot(probs_low, m_heads)
        inner = jnp.sum(grad_probs * probs, axis=0, keepdims=True)
        grad_scores = probs * (grad_probs - inner)
        acc_s[...] += grad_scores
        dland_ref[...] += jnp.sum(grad_scores * land, axis=0, keepdims=True)
        scores_low = grad_scores.astype(BF16)
        grad_q = diagonal(dot(keys.astype(F32).T.astype(BF16), scores_low)).T * scale
        grad_k = dot(scores_low, q_heads) * scale
        grad_packed = jnp.concatenate([grad_q, grad_k, grad_values], axis=1)
        dbin_ref[...] += jnp.sum(grad_packed, axis=0, keepdims=True)
        packed_low = grad_packed.astype(BF16)
        dwin_ref[...] += dot(hidden_f.T.astype(BF16), packed_low)
        grad_hidden = dot(packed_low, win_t_ref[...])
        dgain_ref[...] += jnp.sum(grad_hidden * normed, axis=0, keepdims=True)
        dshift_ref[...] += jnp.sum(grad_hidden, axis=0, keepdims=True)
        scaled = grad_hidden * gain_ref[...]
        grad_tok = inv_std * (
            scaled
            - jnp.mean(scaled, axis=-1, keepdims=True)
            - normed * jnp.mean(scaled * normed, axis=-1, keepdims=True)
        )
        grad_ref[k] = grad_tok.astype(BF16)

    @pl.when(step == pl.num_programs(1) - 1)
    def _():
        dtable_ref[...] = jnp.zeros_like(dtable_ref)
        for h in range(HEADS):
            for j in range(WLON):
                start = h * TL + (WLON - 1 - j) * COL
                dtable_ref[0, :, start : start + WT] += acc_s[
                    j * COL : (j + 1) * COL, h * WT : (h + 1) * WT
                ]


def attend(tokens, cots, land, table, gain, shift, w_in, b_in, w_out, land_gain, bands):
    count = tokens.shape[0]
    windows = count // bands
    per_step = 2 if windows % 2 == 0 else 1
    steps = windows // per_step

    def fixed(shape):
        return pl.BlockSpec(shape, lambda a, w: (0,) * len(shape))

    def per_band(shape):
        return pl.BlockSpec(shape, lambda a, w: (a,) + (0,) * (len(shape) - 1))

    win_spec = pl.BlockSpec((per_step, WT, C), lambda a, w: (a * steps + w, 0, 0))
    shapes = [(C, 3 * C), (1, 3 * C), (C, C), (1, C), (1, C), (1, C), (1, HL)]

    def body(*refs):
        kernel(windows, per_step, *refs)

    return pl.pallas_call(
        body,
        grid=(bands, steps),
        in_specs=[
            win_spec,
            win_spec,
            per_band((1, WT, windows)),
            per_band((1, COL, HEADS * TL)),
            fixed((1, C)),
            fixed((1, C)),
            fixed((C, 3 * C)),
            fixed((3 * C, C)),
            fixed((1, 3 * C)),
            fixed((C, C)),
            fixed((1, HL)),
        ],
        out_specs=[win_spec]
        + [fixed(s) for s in shapes]
        + [per_band((1, COL, HEADS * TL))],
        out_shape=[jax.ShapeDtypeStruct(tokens.shape, BF16)]
        + [jax.ShapeDtypeStruct(s, F32) for s in shapes]
        + [jax.ShapeDtypeStruct((bands, COL, HEADS * TL), F32)],
        scratch_shapes=[pltpu.VMEM((WT, HL), F32), pltpu.VMEM((WT, HL), F32)],
        compiler_params=pltpu.CompilerParams(
            dimension_semantics=("arbitrary", "arbitrary"), vmem_limit_bytes=48 * 1024 * 1024
        ),
    )(
        tokens,
        cots,
        land,
        table,
        gain.reshape(1, C),
        shift.reshape(1, C),
        w_in,
        w_in.T,
        b_in.reshape(1, 3 * C),
        w_out.T,
        jnp.repeat(land_gain, WT).reshape(1, HL),
    )


def normalize_rms(gradient):
    rms_value = jnp.sqrt(jnp.mean(gradient * gradient) + RMS_EPSILON)
    return gradient * (TARGET_RMS / rms_value)


def local(
    sizes,
    states,
    cotangent,
    land_mask,
    pole_mask,
    bias_table,
    norm_gain,
    norm_shift,
    in_weight,
    in_bias,
    out_weight,
    land_gain,
):
    rows = states.shape[1]
    cols = states.shape[2]
    bands = rows // WLAT
    windows = cols // WLON
    both = ("lat", "lon")
    lon_piece = jnp.stack([states[:, :, :S_LON], cotangent[:, :, :S_LON]])
    lat_piece = jnp.stack([states[:, :S_LAT, S_LON:], cotangent[:, :S_LAT, S_LON:]])
    land_low = land_mask.astype(BF16)
    pole_low = pole_mask.astype(BF16)
    lon_rim = moved(lon_piece, "lon", sizes, -1)
    lat_rim = moved(lat_piece, "lat", sizes, -1)
    corner = moved(lon_piece[:, :, :S_LAT], both, sizes, -1)
    land_ahead = jnp.concatenate([land_low[:, S_LON:], moved(land_low[:, :S_LON], "lon", sizes, -1)], axis=1)
    small = jnp.concatenate([land_ahead[:S_LAT], pole_low[:S_LAT, None]], axis=1)
    small_rim = moved(small, "lat", sizes, -1)
    rolled_land = jnp.concatenate([land_ahead[S_LAT:], small_rim[:, :cols]], axis=0).astype(F32)
    rolled_pole = jnp.concatenate([pole_low[S_LAT:], small_rim[:, cols]], axis=0).astype(F32)

    def windowed(own, at):
        top = jnp.concatenate([own[:, S_LAT:, S_LON:], lon_rim[at][:, S_LAT:]], axis=2)
        low = jnp.concatenate([lat_rim[at], corner[at]], axis=2)
        grid = jnp.concatenate([top, low], axis=1)
        return (
            grid.reshape(PL, bands, WLAT, cols, C)
            .transpose(1, 3, 0, 2, 4)
            .reshape(bands * windows, WT, C)
        )

    land_win = rolled_land.reshape(bands, WLAT, windows, WLON).transpose(0, 3, 1, 2)
    land_win = jnp.broadcast_to(
        land_win[:, :, None], (bands, WLON, PL, WLAT, windows)
    ).reshape(bands, WT, windows)
    total_rows = rows * sizes["lat"]
    row_ids = lax.axis_index("lat") * rows + jnp.arange(rows, dtype=jnp.int32)
    part = (row_ids >= total_rows - S_LAT).reshape(bands, WLAT)
    valid = (rolled_pole > 0.5).reshape(bands, WLAT)
    allowed = (part[:, :, None] == part[:, None, :]) & valid[:, :, None]
    table = bias_table.reshape(bands, DL, HEADS, PL, PL, WLAT, WLAT).transpose(0, 4, 6, 2, 1, 3, 5)
    table = jnp.where(allowed[:, None, :, None, None, None, :], table, FAR)
    table = table.reshape(bands, COL, HEADS * TL)
    outs = attend(
        windowed(states, 0),
        windowed(cotangent, 1),
        land_win,
        table,
        norm_gain,
        norm_shift,
        in_weight,
        in_bias,
        out_weight,
        land_gain,
        bands,
    )
    grad_win, dwin, dbin, dwout, dbout, dgain, dshift, dland, dtable = outs
    grad = (
        grad_win.reshape(bands, cols, PL, WLAT, C).transpose(2, 0, 3, 1, 4).reshape(PL, rows, cols, C)
    )
    below = moved(grad[:, rows - S_LAT :, : cols - S_LON], "lat", sizes, 1)
    behind = moved(grad[:, : rows - S_LAT, cols - S_LON :], "lon", sizes, 1)
    back_corner = moved(grad[:, rows - S_LAT :, cols - S_LON :], both, sizes, 1)
    upper = jnp.concatenate([back_corner, below], axis=2)
    lower = jnp.concatenate([behind, grad[:, : rows - S_LAT, : cols - S_LON]], axis=2)
    back = jnp.concatenate([upper, lower], axis=1)
    grad_states = (cotangent.astype(F32) + back.astype(F32)).astype(BF16)
    dland = jnp.sum(dland.reshape(HEADS, WT), axis=1)
    sums = lax.psum((dwin, dbin, dwout, dbout, dgain, dshift, dland), both)
    table_sum = lax.psum(dtable, "lon")
    table_sq = lax.psum(jnp.sum(table_sum * table_sum), "lat")
    table_count = bands * sizes["lat"] * DL * NPOS
    table_rms = jnp.sqrt(table_sq / table_count + RMS_EPSILON)
    table_out = table_sum * (TARGET_RMS / table_rms)
    table_out = table_out.reshape(bands, PL, WLAT, HEADS, DL, PL, WLAT).transpose(0, 4, 3, 5, 1, 6, 2)
    return (
        grad_states,
        normalize_rms(sums[0]),
        normalize_rms(sums[1].reshape(3 * C)),
        normalize_rms(sums[2]),
        normalize_rms(sums[3].reshape(C)),
        normalize_rms(sums[4].reshape(C)),
        normalize_rms(sums[5].reshape(C)),
        normalize_rms(sums[6]),
        table_out.reshape(bands, DL, NPOS),
    )


def solution(mesh):
    sizes = dict(mesh.shape)

    def run(*args):
        return local(sizes, *args)

    return jax.shard_map(
        run,
        mesh=mesh,
        in_specs=(
            P(None, "lat", "lon", None),
            P(None, "lat", "lon", None),
            P("lat", "lon"),
            P("lat"),
            P("lat", None, None),
            P(),
            P(),
            P(),
            P(),
            P(),
            P(),
        ),
        out_specs=(
            P(None, "lat", "lon", None),
            P(),
            P(),
            P(),
            P(),
            P(),
            P(),
            P(),
            P("lat", None, None),
        ),
        check_vma=False,
    )
```

time: 855 us -> 382 us (0.45); the launches traced: 844 us -> 380 us
  local copies, waits for them, and re-layouts: 337 us -> 74.3 us
  matrix products: 209 us -> 0 us
  Pallas kernels: 0 us -> 50.9 us
  other arithmetic: 65.3 us -> 30.2 us
  loops' own time: 30 us -> 0 us
  waiting for transfers between devices: 123 us -> 142 us
    dot_general x39 -> x0, matrix products: 184 us -> none  [the longest x3 83.5 us: collapse_bias(): jnp.einsum('haixbjy,dxy->dhabij', shaped, lon_onehot(), precision=lax.Pre...]
    reshape x9 -> x14, local copies, waits for them, and re-layouts: 148 us -> 48.2 us  [the longest x2 16.7 us: local(): table_out.reshape(bands, PL, WLAT, HEADS, DL, PL, WLAT)]
    add x9 -> x0, local copies, waits for them, and re-layouts: 94.8 us -> none  [the longest x6 94.6 us: window_block(): scores + expand_bias(table_row)[None]]
    pallas_call x0 -> x1, Pallas kernels: none -> 50.9 us  [attend(): pl.pallas_call(body, grid=(bands, steps), in_specs=[win_spec, win_spec, p...]
    psum x2, waiting for transfers between devices: 109 us -> 141 us  [the longest x1 98.5 us: local(): sums = lax.psum((dwin, dbin, dwout, dbout, dgain, dshift, dland), both)]
    another operation x1 -> x0, loops' own time: 30 us -> none  [local(): lax.map(one_band, (tokens_all, cot_all, land_all, row_part, pole_valid, b...]
    dynamic_update_slice x21 -> x0, local copies, waits for them, and re-layouts: 29.9 us -> none  [local(): lax.map(one_band, (tokens_all, cot_all, land_all, row_part, pole_valid, b...]
    sub x3 -> x0, matrix products: 24.6 us -> none  [window_block(): exp_terms = jnp.where(pair_gate, jnp.exp(scores - row_top), 0.0)]
  transfers between devices with their start and end apart: 11 -> 10, of which waited for: 5 -> 3; matrix products, arithmetic and copies ran while one was open for 7% -> 20% of each run, Pallas kernels for 0% -> 0%
where the time goes in v1:
time: 382 us; the launch traced here: 380 us
  waiting for transfers between devices  142 us (37%)
  local copies, waits for them, and re-layouts  74.3 us (19%)
  Pallas kernels  50.9 us (13%)
  blocking collectives  48.6 us (13%)
  other arithmetic  30.2 us (8%)
  between operations  20.1 us (5%)
  starting transfers between devices  13.7 us (4%)
    psum x1, waiting for transfers between devices, local(): sums = lax.psum((dwin, dbin, dwout, dbout, dgain, dshift, dland), both)  98.5 us
    pallas_call x1, Pallas kernels, attend(): pl.pallas_call(body, grid=(bands, steps), in_specs=[win_spec, win_spec, p...  50.9 us
    psum x1, waiting for transfers between devices, local(): table_sum = lax.psum(dtable, 'lon')  42.7 us
    psum x1, blocking collectives, local(): sums = lax.psum((dwin, dbin, dwout, dbout, dgain, dshift, dland), both)  40.2 us
    reshape x2, local copies, waits for them, and re-layouts, local(): table_out.reshape(bands, PL, WLAT, HEADS, DL, PL, WLAT)  16.7 us
    select_n x1, local copies, waits for them, and re-layouts, local(): table = jnp.where(allowed[:, None, :, None, None, None, :], table, FAR)  10.6 us
    ppermute x6, starting transfers between devices, moved(): lax.ppermute(array, axes, [(i, (i + by) % size) for i in range(size)])  9.09 us
    psum x1, blocking collectives, local(): table_sq = lax.psum(jnp.sum(table_sum * table_sum), 'lat')  8.43 us
  transfers between devices with their start and end apart: 10, of which 3 were waited for; matrix products, arithmetic and copies ran while one was open for 20% of the time, Pallas kernels for 0%

profile of v1, /device:TPU:1, one launch (start us, length us, event | category | flops | bytes accessed | tf_op | source)
XLA Modules:
  0.0 380.2 jit_solution(12865704225824980545)
XLA Ops:
  9.5 3.6 collective-permute-start.2
  18.0 3.2 collective-permute-start
  21.8 2.0 slice.91
  25.0 6.1 %reshape.118 = f32[3,11,6,2,2,12,12]{6,5,4,3,2,0,1:T(8,128)} reshape(f32[3,11,3456]{2,0,1:T(4,128)S(1)} %copy-done.8) | data formatting | bytes 912384 | tf_op jit(solution)/shard_map/reshape | solution.py:287
  34.5 7.1 %bitcast_select_fusion = f32[3,2,12,6,11,2,12]{2,6,1,5,3,0,4:T(8,128)} fusion(f32[3,11,6,2,2,12,12]{6,5,4,3,2,0,1:T(8,128)} %reshape.118, pred[3,12,12]{1,2,0:T(8,128)(4,1)S(1)} %compare_and_fusion), kind=kLoop, calls=%fused_computation | loop fusion | flops 114048 | bytes 912816 | tf_op jit(solution)/shard_map/jit(_where)/select_n | solution.py:288
  42.2 10.6 %copy.63 = f32[3,2,12,6,11,2,12]{6,5,4,3,2,1,0:T(2,128)} copy(f32[3,2,12,6,11,2,12]{2,6,1,5,3,0,4:T(8,128)} %bitcast_select_fusion) | data formatting | bytes 912384 | tf_op jit(solution)/shard_map/jit(_where)/select_n | solution.py:288
  52.9 5.2 %reshape.119.refs_3_ = f32[3,24,1584]{2,1,0:T(8,128)S(1)} reshape(f32[3,2,12,6,11,2,12]{6,5,4,3,2,1,0:T(2,128)} %copy.63) | data formatting | bytes 912384 | tf_op jit(solution)/shard_map/reshape | solution.py:289
  62.1 2.2 copy.79
  64.3 4.1 %reshape.116.refs_1_ = bf16[24,144,192]{2,1,0:T(8,128)(2,1)} reshape(bf16[3,48,2,12,192]{4,3,2,1,0:T(8,128)(2,1)} %bitcast.58) | data formatting | bytes 2654208 | tf_op jit(solution)/shard_map/reshape | solution.py:275
  69.4 2.2 copy.80
  71.6 2.9 reshape.114.refs_0_
  74.5 50.9 %shard_map.178 = (bf16[24,144,192]{2,1,0:T(8,128)(2,1)S(1)}, f32[192,576]{1,0:T(8,128)}, f32[1,576]{1,0:T(1,128)S(1)}, f32[192,192]{1,0:T(8,128)}, f32[1,192]{1,...) custom-call(bf16[24,144,192]{2,1,0:T(8,128)(2,1)S(1)} %reshape.114.r, ...), custom_call_target="tpu_custom_call" | custom-call | tf_op jit(solution)/shard_map/pallas_call | solution.py:190
  126.8 40.2 %all-reduce = (f32[1,576]{1,0:T(1,128)S(1)}, f32[1,192]{1,0:T(1,128)S(1)}, f32[1,192]{1,0:T(1,128)S(1)}, f32[1,192]{1,0:T(1,128)S(1)}, f32[6]{0:T(128)S(1)}) all-reduce(f32[1,576]{1,0:T(1,128)S(1)} %get-tuple-element.20, f32[1,192]{1,0:T(1,128)S(1)} %get-tuple-element.22, ...), channel_id=1, replica_groups=mesh['lat'=4,'lon'=8] {'lat','lon'}, use_global_device_ids=true, to_apply=%region_2.3 | all-reduce | flops 1158 | bytes 9264 | tf_op jit(solution)/shard_map/psum | solution.py:315
  173.8 2.8 reshape.123
  180.4 2.1 collective-permute-start.6
  182.5 1.8 collective-permute-start.7
  186.4 42.7 %all-reduce.5.cloned.1.call-done = f32[3,24,1584]{2,1,0:T(8,128)} async-done(((f32[3,24,1584]{2,1,0:T(8,128)}), f32[3,24,1584]{2,1,0:T(8,128)}) %all-reduce.5.cloned.1.call-update) | async-done | bytes 456208 | tf_op jit(solution)/shard_map/psum | solution.py:316
  230.9 3.2 add_convert_fusion
  234.1 8.4 %psum.71 = f32[]{:T(128)} all-reduce(f32[]{:T(128)} %multiply_reduce_fusion.1), channel_id=1, replica_groups=mesh['lat'=4,'lon'=8] {'lat'}, use_global_device_ids=true, to_apply=%region_17.18 | all-reduce | flops 1 | bytes 8 | tf_op jit(solution)/shard_map/psum | solution.py:317
  244.3 6.3 %reshape.126 = f32[3,2,12,6,11,2,12]{6,5,4,3,2,1,0:T(2,128)} reshape(f32[3,24,1584]{2,1,0:T(8,128)S(1)} %broadcast_multiply_fusion.1) | data formatting | bytes 912384 | tf_op jit(solution)/shard_map/reshape | solution.py:321
  250.6 10.4 %copy.68 = f32[3,2,12,6,11,2,12]{2,6,1,5,3,0,4:T(8,128)} copy(f32[3,2,12,6,11,2,12]{6,5,4,3,2,1,0:T(2,128)} %reshape.126) | data formatting | bytes 912384 | tf_op jit(solution)/shard_map/reshape | solution.py:321
  261.0 5.7 %reshape.127 = f32[3,11,3456]{2,0,1:T(4,128)} reshape(f32[3,11,6,2,2,12,12]{6,5,4,3,2,0,1:T(8,128)} %bitcast.57) | data formatting | bytes 912384 | tf_op jit(solution)/shard_map/reshape | solution.py:331
  266.7 98.5 %all-reduce.7.cloned.1.call-done = (f32[192,576]{1,0:T(8,128)}, f32[192,192]{1,0:T(8,128)}) async-done(((f32[192,576]{1,0:T(8,128)}, f32[192,192]{1,0:T(8,128)}), (f32[192,576]{1,0:T(8,128)}, f32[192,192]{1,0:T(8,128)})) %all-reduce.7.cloned.1.call-update) | async-done | bytes 589840 | tf_op jit(solution)/shard_map/psum | solution.py:315
  371.5 1.8 broadcast_multiply_fusion
  (115 shorter events, 36.2 us)
Async XLA Ops:
  7.2 222.0 %all-reduce.5.cloned.1.call-start = ((), (), s32[]{:S(2)}) async-start(), calls=%async_computation | async-start | bytes 958464 | tf_op jit(solution)/shard_map/psum | solution.py:316
  9.2 12.0 %copy-start.10 = (s32[36,48]{1,0:T(8,128)S(1)}, s32[36,48]{1,0:T(8,128)}, u32[]{:S(2)}) copy-start(s32[36,48]{1,0:T(8,128)} %param.13) | copy-start | bytes 20740
  9.2 12.6 %copy-start.4 = (bf16[2,36,48,192]{3,2,1,0:T(8,128)(2,1)S(1)}, bf16[2,36,48,192]{3,2,1,0:T(8,128)(2,1)}, u32[]{:S(2)}) copy-start(bf16[2,36,48,192]{3,2,1,0:T(8,128)(2,1)} %param.12) | copy-start | bytes 3981316
  9.5 48.6 %collective-permute-start.2 = (bf16[2,2,6,3,192]{4,1,3,2,0:T(2,128)(2,1)S(1)}, bf16[2,2,6,3,192]{4,1,3,2,0:T(2,128)(2,1)S(1)}, u32[]{:S(2)}, u32[]{:S(2)}) collective-permute-start(bf16[2,2,6,3,192]{4,1,3,2,0:T(2,128)(2,1)S(1)} %fusion), channel_id=1, source_target_pairs={{0,31},{1,24},{2,25},{3,26},{4,27},{5,28},{6,29},{7,30},{8,7},{9,0... | collective-permute-start | bytes 82952 | tf_op jit(solution)/shard_map/ppermute | solution.py:41
  15.8 8.0 %copy-start.7 = (bf16[2,36,48,192]{3,2,1,0:T(8,128)(2,1)S(1)}, bf16[2,36,48,192]{3,2,1,0:T(8,128)(2,1)}, u32[]{:S(2)}) copy-start(bf16[2,36,48,192]{3,2,1,0:T(8,128)(2,1)} %param.11) | copy-start | bytes 3981316
  16.7 42.9 %collective-permute-start.1 = (bf16[2,2,6,45,192]{4,1,3,2,0:T(2,128)(2,1)S(1)}, bf16[2,2,6,45,192]{4,1,3,2,0:T(2,128)(2,1)}, u32[]{:S(2)}, u32[]{:S(2)}) collective-permute-start(bf16[2,2,6,45,192]{4,1,3,2,0:T(2,128)(2,1)S(1)} %pad_maximum_fusion.2), channel_id=1, source_target_pairs={{0,24},{8,0},{16,8},{24,16},{1,25},{9,1},{17,9},{25,17},{2,26},{10... | collective-permute-start | bytes 1244168 | tf_op jit(solution)/shard_map/ppermute | solution.py:34
  18.0 40.1 %collective-permute-start = (bf16[2,2,36,3,192]{4,1,3,2,0:T(2,128)(2,1)}, bf16[2,2,36,3,192]{4,1,3,2,0:T(2,128)(2,1)}, u32[]{:S(2)}, u32[]{:S(2)}) collective-permute-start(bf16[2,2,36,3,192]{4,1,3,2,0:T(2,128)(2,1)} %pad_maximum_fusion.5), channel_id=1, source_target_pairs={{0,7},{1,0},{2,1},{3,2},{4,3},{5,4},{6,5},{7,6},{8,15},{9,8},{10,9... | collective-permute-start | bytes 497672 | tf_op jit(solution)/shard_map/ppermute | solution.py:34
  21.2 3.5 copy-start.13
  21.2 3.7 copy-start.8
  21.2 10.3 %collective-permute-start.3 = (bf16[36,3]{1,0:T(8,128)(2,1)S(1)}, bf16[36,3]{1,0:T(8,128)(2,1)S(1)}, u32[]{:S(2)}, u32[]{:S(2)}) collective-permute-start(bf16[36,3]{1,0:T(8,128)(2,1)S(1)} %bitcast.68), channel_id=1, source_target_pairs={{0,7},{1,0},{2,1},{3,2},{4,3},{5,4},{6,5},{7,6},{8,15},{9,8},{10,9... | collective-permute-start | bytes 656 | tf_op jit(solution)/shard_map/ppermute | solution.py:34
  25.0 6.1 %copy-start.1 = (bf16[192,576]{1,0:T(8,128)(2,1)S(1)}, bf16[192,576]{1,0:T(8,128)(2,1)}, u32[]{:S(2)}) copy-start(bf16[192,576]{1,0:T(8,128)(2,1)} %refs_6_.1) | copy-start | bytes 663556
  25.0 6.3 %copy-start.9 = (bf16[192,192]{1,0:T(8,128)(2,1)S(1)}, bf16[192,192]{1,0:T(8,128)(2,1)}, u32[]{:S(2)}) copy-start(bf16[192,192]{1,0:T(8,128)(2,1)} %param.20) | copy-start | bytes 221188
  25.0 6.4 %copy-start.12 = (f32[6]{0:T(128)S(1)}, f32[6]{0:T(128)}, u32[]{:S(2)}) copy-start(f32[6]{0:T(128)} %param.21) | copy-start | bytes 76
  25.0 6.5 %copy-start.11 = (f32[576]{0:T(1024)S(1)}, f32[576]{0:T(1024)}, u32[]{:S(2)}) copy-start(f32[576]{0:T(1024)} %param.19) | copy-start | bytes 6916
  31.6 2.4 collective-permute-start.4
  58.1 3.4 copy-start.6
  71.6 2.9 copy-start.2
  71.6 2.9 copy-start.3
  125.4 1.2 copy-start
  173.2 192.0 %all-reduce.7.cloned.1.call-start = ((), (), s32[]{:S(2)}) async-start(), calls=%async_computation.1 | async-start | bytes 1376256 | tf_op jit(solution)/shard_map/psum | solution.py:315
  177.6 53.3 %copy-start.5 = (bf16[2,36,48,192]{3,2,1,0:T(8,128)(2,1)S(1)}, bf16[2,36,48,192]{3,2,1,0:T(8,128)(2,1)}, u32[]{:S(2)}) copy-start(bf16[2,36,48,192]{3,2,1,0:T(8,128)(2,1)} %param.12) | copy-start | bytes 3981316
  180.4 50.5 %collective-permute-start.6 = (bf16[2,6,45,192]{3,2,1,0:T(8,128)(2,1)S(1)}, bf16[2,6,45,192]{3,2,1,0:T(8,128)(2,1)}, u32[]{:S(2)}, u32[]{:S(2)}) collective-permute-start(bf16[2,6,45,192]{3,2,1,0:T(8,128)(2,1)S(1)} %slice.123), channel_id=1, source_target_pairs={{0,8},{8,16},{16,24},{24,0},{1,9},{9,17},{17,25},{25,1},{2,10},{10... | collective-permute-start | bytes 622088 | tf_op jit(solution)/shard_map/ppermute | solution.py:34
  182.5 48.4 %collective-permute-start.7 = (bf16[2,30,3,192]{3,2,1,0:T(4,128)(2,1)}, bf16[2,30,3,192]{3,2,1,0:T(4,128)(2,1)}, u32[]{:S(2)}, u32[]{:S(2)}) collective-permute-start(bf16[2,30,3,192]{3,2,1,0:T(4,128)(2,1)} %slice.124), channel_id=1, source_target_pairs={{0,1},{1,2},{2,3},{3,4},{4,5},{5,6},{6,7},{7,0},{8,9},{9,10},{10,1... | collective-permute-start | bytes 207368 | tf_op jit(solution)/shard_map/ppermute | solution.py:34
  184.3 46.6 %collective-permute-start.5 = (bf16[2,6,3,192]{3,2,1,0:T(4,128)(2,1)}, bf16[2,6,3,192]{3,2,1,0:T(4,128)(2,1)}, u32[]{:S(2)}, u32[]{:S(2)}) collective-permute-start(bf16[2,6,3,192]{3,2,1,0:T(4,128)(2,1)} %slice.122), channel_id=1, source_target_pairs={{0,9},{1,10},{2,11},{3,12},{4,13},{5,14},{6,15},{7,8},{8,17},{9,18... | collective-permute-start | bytes 41480 | tf_op jit(solution)/shard_map/ppermute | solution.py:41
Sparse Core Ops, SparseCore 0:
  173.3 55.8 all-reduce.4
  235.9 129.2 all-reduce.6

commit v2 on v1

--- a/solution.py
+++ b/solution.py
@@ -1,3 +1,5 @@
+import functools
+
 import jax
 import jax.numpy as jnp
 from jax import lax
@@ -19,6 +21,9 @@
 COL = PL * WLAT
 HL = HEADS * WT
 TL = DL * COL
+TW = -(-HEADS * TL // 128)
+HB = NPOS // HEADS
+SMALL = 24
 
 EPSILON = 1e-05
 TARGET_RMS = 0.5
@@ -57,6 +62,18 @@
     return jnp.concatenate(
         [full[HD * h : HD * (h + 1), WT * h : WT * (h + 1)] for h in range(HEADS)], axis=0
     )
+
+
+def table_masks():
+    row = lax.broadcasted_iota(jnp.int32, (COL, HB), 0)
+    place = lax.broadcasted_iota(jnp.int32, (COL, HB), 1)
+    q_level = place // (HB // 2)
+    k_level = place // WT % 2
+    q_row = place // WLAT % WLAT
+    k_row = place % WLAT
+    keep = (row == q_level * WLAT + q_row).astype(F32)
+    pick = (row == k_level * WLAT + k_row).astype(F32)
+    return keep, pick
 
 
 def kernel(
@@ -73,7 +90,11 @@
     bin_ref,
     wout_t_ref,
     lg_ref,
+    gate_ref,
     grad_ref,
+    dense_ref,
+    small_ref,
+    dtable_ref,
     dwin_ref,
     dbin_ref,
     dwout_ref,
@@ -81,9 +102,9 @@
     dgain_ref,
     dshift_ref,
     dland_ref,
-    dtable_ref,
     bias_s,
     acc_s,
+    fold_s,
 ):
     band = pl.program_id(0)
     step = pl.program_id(1)
@@ -97,11 +118,25 @@
     @pl.when(step == 0)
     def _():
         acc_s[...] = jnp.zeros_like(acc_s)
+        keep, pick = table_masks()
+        for h in range(HEADS):
+            own = table_ref[0, :, h * HB : (h + 1) * HB]
+            spread = (own[:, None, :] * keep[None]).reshape(TL, HB)
+            fold_s[:, h * TL : (h + 1) * TL] = (
+                lax.dot_general(
+                    pick,
+                    spread,
+                    (((1,), (1,)), ((), ())),
+                    precision=lax.Precision.HIGHEST,
+                    preferred_element_type=F32,
+                )
+                + gate_ref[0]
+            )
         for h in range(HEADS):
             for j in range(WLON):
                 start = h * TL + (WLON - 1 - j) * COL
-                bias_s[j * COL : (j + 1) * COL, h * WT : (h + 1) * WT] = table_ref[
-                    0, :, start : start + WT
+                bias_s[j * COL : (j + 1) * COL, h * WT : (h + 1) * WT] = fold_s[
+                    :, start : start + WT
                 ]
 
     lane = lax.broadcasted_iota(jnp.int32, (1, C), 1) // HD
@@ -160,16 +195,34 @@
 
     @pl.when(step == pl.num_programs(1) - 1)
     def _():
-        dtable_ref[...] = jnp.zeros_like(dtable_ref)
+        fold_s[...] = jnp.zeros_like(fold_s)
         for h in range(HEADS):
             for j in range(WLON):
                 start = h * TL + (WLON - 1 - j) * COL
-                dtable_ref[0, :, start : start + WT] += acc_s[
+                fold_s[:, start : start + WT] += acc_s[
                     j * COL : (j + 1) * COL, h * WT : (h + 1) * WT
                 ]
-
-
-def attend(tokens, cots, land, table, gain, shift, w_in, b_in, w_out, land_gain, bands):
+        for t in range(TW):
+            dtable_ref[t, pl.ds(pl.multiple_of(band * COL, COL), COL), :] = fold_s[
+                :, t * 128 : (t + 1) * 128
+            ]
+
+    @pl.when((band == pl.num_programs(0) - 1) & (step == pl.num_programs(1) - 1))
+    def _():
+        dense = jnp.concatenate([dwin_ref[...], dwout_ref[...]], axis=1)
+        for t in range(4 * C // 128):
+            dense_ref[t] = dense[:, t * 128 : (t + 1) * 128]
+        small_ref[...] = jnp.zeros_like(small_ref)
+        at = 0
+        for ref in (dbin_ref, dbout_ref, dgain_ref, dshift_ref, dland_ref):
+            width = ref.shape[1]
+            for start in range(0, width, 128):
+                size = min(128, width - start)
+                small_ref[at : at + 1, :size] = ref[:, start : start + size]
+                at += 1
+
+
+def attend(tokens, cots, land, table, gate, gain, shift, w_in, b_in, w_out, land_gain, bands):
     count = tokens.shape[0]
     windows = count // bands
     per_step = 2 if windows % 2 == 0 else 1
@@ -183,6 +236,7 @@
 
     win_spec = pl.BlockSpec((per_step, WT, C), lambda a, w: (a * steps + w, 0, 0))
     shapes = [(C, 3 * C), (1, 3 * C), (C, C), (1, C), (1, C), (1, C), (1, HL)]
+    tiles = [(4 * C // 128, C, 128), (SMALL, 128), (TW, bands * COL, 128)]
 
     def body(*refs):
         kernel(windows, per_step, *refs)
@@ -194,7 +248,7 @@
             win_spec,
             win_spec,
             per_band((1, WT, windows)),
-            per_band((1, COL, HEADS * TL)),
+            per_band((1, DL, NPOS)),
             fixed((1, C)),
             fixed((1, C)),
             fixed((C, 3 * C)),
@@ -202,14 +256,13 @@
             fixed((1, 3 * C)),
             fixed((C, C)),
             fixed((1, HL)),
+            per_band((1, COL, TL)),
         ],
-        out_specs=[win_spec]
-        + [fixed(s) for s in shapes]
-        + [per_band((1, COL, HEADS * TL))],
+        out_specs=[win_spec] + [fixed(t) for t in tiles],
         out_shape=[jax.ShapeDtypeStruct(tokens.shape, BF16)]
-        + [jax.ShapeDtypeStruct(s, F32) for s in shapes]
-        + [jax.ShapeDtypeStruct((bands, COL, HEADS * TL), F32)],
-        scratch_shapes=[pltpu.VMEM((WT, HL), F32), pltpu.VMEM((WT, HL), F32)],
+        + [jax.ShapeDtypeStruct(t, F32) for t in tiles],
+        scratch_shapes=[pltpu.VMEM(t, F32) for t in shapes]
+        + [pltpu.VMEM((WT, HL), F32), pltpu.VMEM((WT, HL), F32), pltpu.VMEM((COL, TW * 128), F32)],
         compiler_params=pltpu.CompilerParams(
             dimension_semantics=("arbitrary", "arbitrary"), vmem_limit_bytes=48 * 1024 * 1024
         ),
@@ -225,7 +278,260 @@
         b_in.reshape(1, 3 * C),
         w_out.T,
         jnp.repeat(land_gain, WT).reshape(1, HL),
-    )
+        gate,
+    )
+
+
+def ceil_to(n, m):
+    return -(-n // m) * m
+
+
+def exchange_kernel(
+    n_lat,
+    n_lon,
+    t_chunk,
+    d_chunk,
+    dense_ref,
+    small_ref,
+    table_ref,
+    dense_out,
+    small_out,
+    table_out,
+    sq_out,
+    s_lat,
+    s_lon,
+    d_own,
+    t_own,
+    d_lat,
+    d_lon,
+    t_lon,
+    d_part,
+    d_all,
+    t_all,
+    sq,
+    lat_send,
+    lat_recv,
+    dl_send,
+    dl_recv,
+    tl_send,
+    tl_recv,
+    dg_send,
+    dg_recv,
+    tg_send,
+    tg_recv,
+    lg_send,
+    lg_recv,
+    sq_send,
+    sq_recv,
+    sl_send,
+    sl_recv,
+    so_send,
+    so_recv,
+):
+    lat = lax.axis_index("lat")
+    lon = lax.axis_index("lon")
+    quarter = n_lon * d_chunk
+    lat_peers = [(k, lax.rem(lat + k, n_lat)) for k in range(1, n_lat)]
+    lon_peers = [(k, lax.rem(lon + k, n_lon)) for k in range(1, n_lon)]
+
+    def rows(index, size):
+        return pl.ds(pl.multiple_of(index * size, size), size)
+
+    def send(src, dst, sends, recvs, k, target):
+        copy = pltpu.make_async_remote_copy(
+            src_ref=src,
+            dst_ref=dst,
+            send_sem=sends.at[k],
+            recv_sem=recvs.at[k],
+            device_id=target,
+            device_id_type=pl.DeviceIdType.MESH,
+        )
+        copy.start()
+        return copy
+
+    barrier = pltpu.get_barrier_semaphore()
+    for _, peer in lat_peers:
+        pl.semaphore_signal(
+            barrier, inc=1, device_id=(peer, lon), device_id_type=pl.DeviceIdType.MESH
+        )
+    for _, peer in lon_peers:
+        pl.semaphore_signal(
+            barrier, inc=1, device_id=(lat, peer), device_id_type=pl.DeviceIdType.MESH
+        )
+    d_rows = dense_ref.shape[0]
+    t_rows = table_ref.shape[0]
+    d_own[0:d_rows] = dense_ref[...].astype(BF16)
+    if d_own.shape[0] > d_rows:
+        d_own[d_rows:] = jnp.zeros((d_own.shape[0] - d_rows, 128), BF16)
+    s_lat[lat] = small_ref[...]
+    t_even = ceil_to(t_rows, 16)
+    table = table_ref[...]
+    if t_even > t_rows:
+        table = jnp.concatenate([table, jnp.zeros((t_even - t_rows, 128), F32)], axis=0)
+    t_own[0:t_even] = table.astype(BF16)
+    if t_own.shape[0] > t_even:
+        t_own[t_even:] = jnp.zeros((t_own.shape[0] - t_even, 128), BF16)
+    pl.semaphore_wait(barrier, n_lat + n_lon - 2)
+
+    s_copies = [
+        send(s_lat.at[lat], s_lat.at[lat], sl_send, sl_recv, k - 1, (p, lon)) for k, p in lat_peers
+    ]
+    lat_copies = [
+        send(d_own.at[rows(p, quarter)], d_lat.at[k - 1], lat_send, lat_recv, k - 1, (p, lon))
+        for k, p in lat_peers
+    ]
+    t_copies = [
+        send(t_own.at[rows(p, t_chunk)], t_lon.at[k - 1], tl_send, tl_recv, k - 1, (lat, p))
+        for k, p in lon_peers
+    ]
+    for copy in s_copies:
+        copy.wait()
+    s_lon[lon] = functools.reduce(jnp.add, [s_lat[i] for i in range(n_lat)])
+    so_copies = [
+        send(s_lon.at[lon], s_lon.at[lon], so_send, so_recv, k - 1, (lat, p)) for k, p in lon_peers
+    ]
+    for copy in lat_copies:
+        copy.wait()
+    total = d_own[rows(lat, quarter)].astype(F32)
+    for k, _ in lat_peers:
+        total = total + d_lat[k - 1].astype(F32)
+    d_part[...] = total.astype(BF16)
+    d_copies = [
+        send(d_part.at[rows(p, d_chunk)], d_lon.at[k - 1], dl_send, dl_recv, k - 1, (lat, p))
+        for k, p in lon_peers
+    ]
+    for copy in t_copies:
+        copy.wait()
+    total = t_own[rows(lon, t_chunk)].astype(F32)
+    for k, _ in lon_peers:
+        total = total + t_lon[k - 1].astype(F32)
+    t_mine = rows(lon, t_chunk)
+    t_all[t_mine] = total.astype(BF16)
+    tg_copies = [
+        send(t_all.at[t_mine], t_all.at[t_mine], tg_send, tg_recv, k - 1, (lat, p))
+        for k, p in lon_peers
+    ]
+    for copy in d_copies:
+        copy.wait()
+    total = d_part[rows(lon, d_chunk)].astype(F32)
+    for k, _ in lon_peers:
+        total = total + d_lon[k - 1].astype(F32)
+    d_mine = rows(lat * n_lon + lon, d_chunk)
+    d_all[d_mine] = total.astype(BF16)
+    dg_copies = [
+        send(d_all.at[d_mine], d_all.at[d_mine], dg_send, dg_recv, k - 1, (lat, p))
+        for k, p in lon_peers
+    ]
+    for copy in tg_copies:
+        copy.wait()
+    summed = t_all[...].astype(F32)
+    sq[0] = jnp.sum((summed * summed).reshape(summed.shape[0] // 8, 8, 128), axis=0)
+    sq_copies = [
+        send(sq.at[0], sq.at[k], sq_send, sq_recv, k - 1, (p, lon)) for k, p in lat_peers
+    ]
+    for copy in dg_copies:
+        copy.wait()
+    mine = rows(lat, quarter)
+    lg_copies = [
+        send(d_all.at[mine], d_all.at[mine], lg_send, lg_recv, k - 1, (p, lon))
+        for k, p in lat_peers
+    ]
+    table_out[...] = summed
+    for copy in sq_copies:
+        copy.wait()
+    squares = sq[0]
+    for k, _ in lat_peers:
+        squares = squares + sq[k]
+    sq_out[...] = squares
+    for copy in so_copies:
+        copy.wait()
+    small_out[...] = functools.reduce(jnp.add, [s_lon[i] for i in range(n_lon)])
+    for copy in lg_copies:
+        copy.wait()
+    dense_out[...] = d_all[...].astype(F32)
+
+
+def exchange(sizes, dense, small, table):
+    n_lat, n_lon = sizes["lat"], sizes["lon"]
+    t_chunk = ceil_to(-(-table.shape[0] // n_lon), 16)
+    d_chunk = ceil_to(-(-dense.shape[0] // (n_lat * n_lon)), 16)
+    t_total = n_lon * t_chunk
+    d_total = n_lat * n_lon * d_chunk
+    vmem = pl.BlockSpec(memory_space=pltpu.VMEM)
+
+    def body(*refs):
+        exchange_kernel(n_lat, n_lon, t_chunk, d_chunk, *refs)
+
+    def sems(n):
+        return [pltpu.SemaphoreType.DMA((n - 1,))] * 2
+
+    return pl.pallas_call(
+        body,
+        in_specs=[vmem] * 3,
+        out_specs=[vmem] * 4,
+        out_shape=[
+            jax.ShapeDtypeStruct((d_total, 128), F32),
+            jax.ShapeDtypeStruct((SMALL, 128), F32),
+            jax.ShapeDtypeStruct((t_total, 128), F32),
+            jax.ShapeDtypeStruct((8, 128), F32),
+        ],
+        scratch_shapes=[
+            pltpu.VMEM((n_lat, SMALL, 128), F32),
+            pltpu.VMEM((n_lon, SMALL, 128), F32),
+            pltpu.VMEM((d_total, 128), BF16),
+            pltpu.VMEM((t_total, 128), BF16),
+            pltpu.VMEM((n_lat - 1, n_lon * d_chunk, 128), BF16),
+            pltpu.VMEM((n_lon - 1, d_chunk, 128), BF16),
+            pltpu.VMEM((n_lon - 1, t_chunk, 128), BF16),
+            pltpu.VMEM((n_lon * d_chunk, 128), BF16),
+            pltpu.VMEM((d_total, 128), BF16),
+            pltpu.VMEM((t_total, 128), BF16),
+            pltpu.VMEM((n_lat, 8, 128), F32),
+        ]
+        + sems(n_lat)
+        + sems(n_lon) * 4
+        + sems(n_lat) * 3
+        + sems(n_lon),
+        compiler_params=pltpu.CompilerParams(
+            collective_id=0, has_side_effects=True, vmem_limit_bytes=48 * 1024 * 1024
+        ),
+    )(dense, small, table)
+
+
+def collapse_kernel(bands, count, table_ref, sq_ref, out_ref, fold_s):
+    keep, pick = table_masks()
+    total = jnp.sum(jnp.sum(sq_ref[...], axis=0, keepdims=True), axis=1, keepdims=True)
+    factor = TARGET_RMS / jnp.sqrt(total / count + RMS_EPSILON)
+    for band in range(bands):
+        for t in range(TW):
+            start = t * bands * COL + band * COL
+            fold_s[:, t * 128 : (t + 1) * 128] = table_ref[start : start + COL]
+        for h in range(HEADS):
+            part = lax.dot_general(
+                fold_s[:, h * TL : (h + 1) * TL].T * factor,
+                pick,
+                (((1,), (0,)), ((), ())),
+                precision=lax.Precision.HIGHEST,
+                preferred_element_type=F32,
+            )
+            part = part.reshape(DL, COL, HB) * keep[None]
+            out_ref[band, :, h * HB : (h + 1) * HB] = jnp.sum(part, axis=1)
+
+
+def collapse(bands, count, table, squares):
+    vmem = pl.BlockSpec(memory_space=pltpu.VMEM)
+
+    def body(*refs):
+        collapse_kernel(bands, count, *refs)
+
+    return pl.pallas_call(
+        body,
+        in_specs=[vmem] * 2,
+        out_specs=vmem,
+        out_shape=jax.ShapeDtypeStruct((bands, DL, NPOS), F32),
+        scratch_shapes=[pltpu.VMEM((COL, TW * 128), F32)],
+        compiler_params=pltpu.CompilerParams(vmem_limit_bytes=48 * 1024 * 1024),
+    )(table, squares)
 
 
 def normalize_rms(gradient):
@@ -284,14 +590,14 @@
     part = (row_ids >= total_rows - S_LAT).reshape(bands, WLAT)
     valid = (rolled_pole > 0.5).reshape(bands, WLAT)
     allowed = (part[:, :, None] == part[:, None, :]) & valid[:, :, None]
-    table = bias_table.reshape(bands, DL, HEADS, PL, PL, WLAT, WLAT).transpose(0, 4, 6, 2, 1, 3, 5)
-    table = jnp.where(allowed[:, None, :, None, None, None, :], table, FAR)
-    table = table.reshape(bands, COL, HEADS * TL)
+    gate = jnp.where(allowed[:, None, :, None, None, :], 0.0, FAR)
+    gate = jnp.broadcast_to(gate, (bands, PL, WLAT, DL, PL, WLAT)).reshape(bands, COL, TL)
     outs = attend(
         windowed(states, 0),
         windowed(cotangent, 1),
         land_win,
-        table,
+        bias_table,
+        gate,
         norm_gain,
         norm_shift,
         in_weight,
@@ -300,7 +606,7 @@
         land_gain,
         bands,
     )
-    grad_win, dwin, dbin, dwout, dbout, dgain, dshift, dland, dtable = outs
+    grad_win, dense, small, dtable = outs
     grad = (
         grad_win.reshape(bands, cols, PL, WLAT, C).transpose(2, 0, 3, 1, 4).reshape(PL, rows, cols, C)
     )
@@ -311,24 +617,32 @@
     lower = jnp.concatenate([behind, grad[:, : rows - S_LAT, : cols - S_LON]], axis=2)
     back = jnp.concatenate([upper, lower], axis=1)
     grad_states = (cotangent.astype(F32) + back.astype(F32)).astype(BF16)
-    dland = jnp.sum(dland.reshape(HEADS, WT), axis=1)
-    sums = lax.psum((dwin, dbin, dwout, dbout, dgain, dshift, dland), both)
-    table_sum = lax.psum(dtable, "lon")
-    table_sq = lax.psum(jnp.sum(table_sum * table_sum), "lat")
+    dense_sum, small_sum, table_sum, table_sq = exchange(
+        sizes, dense.reshape(-1, 128), small, dtable.reshape(-1, 128)
+    )
     table_count = bands * sizes["lat"] * DL * NPOS
-    table_rms = jnp.sqrt(table_sq / table_count + RMS_EPSILON)
-    table_out = table_sum * (TARGET_RMS / table_rms)
-    table_out = table_out.reshape(bands, PL, WLAT, HEADS, DL, PL, WLAT).transpose(0, 4, 3, 5, 1, 6, 2)
+    table_out = collapse(bands, table_count, table_sum, table_sq)
+    dense_rows = 4 * C // 128 * C
+    both_weights = (
+        dense_sum[:dense_rows].reshape(4 * C // 128, C, 128).transpose(1, 0, 2).reshape(C, 4 * C)
+    )
+    vectors = []
+    at = 0
+    for width in (3 * C, C, C, C, HL):
+        count = -(-width // 128)
+        vectors.append(small_sum[at : at + count].reshape(-1)[:width])
+        at += count
+    dland = jnp.sum(vectors[4].reshape(HEADS, WT), axis=1)
     return (
         grad_states,
-        normalize_rms(sums[0]),
-        normalize_rms(sums[1].reshape(3 * C)),
-        normalize_rms(sums[2]),
-        normalize_rms(sums[3].reshape(C)),
-        normalize_rms(sums[4].reshape(C)),
-        normalize_rms(sums[5].reshape(C)),
-        normalize_rms(sums[6]),
-        table_out.reshape(bands, DL, NPOS),
+        normalize_rms(both_weights[:, : 3 * C]),
+        normalize_rms(vectors[0]),
+        normalize_rms(both_weights[:, 3 * C :]),
+        normalize_rms(vectors[1]),
+        normalize_rms(vectors[2]),
+        normalize_rms(vectors[3]),
+        normalize_rms(dland),
+        table_out,
     )
 
 

time: 382 us -> 179 us (0.47)
  waiting for transfers between devices: 142 us -> 7.98 us
  Pallas kernels: 50.9 us -> 101 us
  blocking collectives: 48.6 us -> 0 us
  local copies, waits for them, and re-layouts: 74.3 us -> 33.6 us
  between operations: 20.1 us -> 5.93 us
  other arithmetic: 30.2 us -> 17 us
    psum x2 -> x0, waiting for transfers between devices: 141 us -> none  [the longest x1 98.5 us: local(): sums = lax.psum((dwin, dbin, dwout, dbout, dgain, dshift, dland), both)]
    psum x2 -> x0, blocking collectives: 48.6 us -> none  [the longest x1 40.2 us: local(): sums = lax.psum((dwin, dbin, dwout, dbout, dgain, dshift, dland), both)]
    pallas_call x0 -> x2, Pallas kernels: none -> 39.6 us  [the longest x1 27.9 us: exchange(): pl.pallas_call(body, in_specs=[vmem] * 3, out_specs=[vmem] * 4, out_shape...]
    reshape x6, local copies, waits for them, and re-layouts: 33.7 us -> 2.09 us  [the longest x1 1.65 us: local(): jnp.broadcast_to(gate, (bands, PL, WLAT, DL, PL, WLAT))]
    select_n x1 -> x0, local copies, waits for them, and re-layouts: 10.6 us -> none  [local(): table = jnp.where(allowed[:, None, :, None, None, None, :], table, FAR)]
    pallas_call x1, Pallas kernels: 50.9 us -> 61.3 us  [attend(): pl.pallas_call(body, grid=(bands, steps), in_specs=[win_spec, win_spec, p...]
    select_n x1, other arithmetic: 7.14 us -> 0.08 us  [local(): gate = jnp.where(allowed[:, None, :, None, None, :], 0.0, FAR)]
    ppermute x6, waiting for transfers between devices: 1.21 us -> 7.98 us  [moved(): lax.ppermute(array, axes, [(i, (i + by) % size) for i in range(size)])]
  transfers between devices with their start and end apart: 10 -> 8, of which waited for: 3 -> 1; matrix products, arithmetic and copies ran while one was open for 20% -> 10% of each run, Pallas kernels for 0% -> 7%
where the time goes in v2:
time: 179 us; the launch traced here: 177 us
  Pallas kernels  101 us (56%)
  local copies, waits for them, and re-layouts  33.6 us (19%)
  other arithmetic  17 us (9%)
  starting transfers between devices  12.1 us (7%)
  waiting for transfers between devices  7.98 us (4%)
  between operations  5.93 us (3%)
    pallas_call x1, Pallas kernels, attend(): pl.pallas_call(body, grid=(bands, steps), in_specs=[win_spec, win_spec, p...  61.3 us
    pallas_call x1, Pallas kernels, exchange(): pl.pallas_call(body, in_specs=[vmem] * 3, out_specs=[vmem] * 4, out_shape...  27.9 us
    pallas_call x1, Pallas kernels, collapse(): pl.pallas_call(body, in_specs=[vmem] * 2, out_specs=vmem, out_shape=jax.S...  11.7 us
    ppermute x2, starting transfers between devices, moved(): return lax.ppermute(array, axes, pairs)  8.87 us
    reshape x2, local copies, waits for them, and re-layouts, windowed(): return grid.reshape(PL, bands, WLAT, cols, C).transpose(1, 3, 0, 2, 4).re...  8.32 us
    ppermute x6, waiting for transfers between devices, moved(): lax.ppermute(array, axes, [(i, (i + by) % size) for i in range(size)])  7.98 us
    reduce_sum x7, other arithmetic, normalize_rms(): rms_value = jnp.sqrt(jnp.mean(gradient * gradient) + RMS_EPSILON)  4.45 us
    mul x7, other arithmetic, normalize_rms(): return gradient * (TARGET_RMS / rms_value)  4.41 us
  transfers between devices with their start and end apart: 8, of which 1 were waited for; matrix products, arithmetic and copies ran while one was open for 10% of the time, Pallas kernels for 7%

profile of v2, /device:TPU:1, one launch (start us, length us, event | category | flops | bytes accessed | tf_op | source)
XLA Modules:
  0.0 177.5 jit_solution(14728177757389787956)
XLA Ops:
  3.9 6.6 %collective-permute-start.2 = (bf16[2,2,6,3,192]{4,1,3,2,0:T(2,128)(2,1)S(1)}, bf16[2,2,6,3,192]{4,1,3,2,0:T(2,128)(2,1)S(1)}, u32[]{:S(2)}, u32[]{:S(2)}) collective-permute-start(bf16[2,2,6,3,192]{4,1,3,2,0:T(2,128)(2,1)S(1)} %fusion), channel_id=1, source_target_pairs={{0,31},{1,24},{2,25},{3,26},{4,27},{5,28},{6,29},{7,30},{8,7},{9,0... | collective-permute-start | bytes 82952 | tf_op jit(solution)/shard_map/ppermute | solution.py:46
  10.4 1.0 pad_maximum_fusion.5
  12.0 1.1 slice.125
  13.7 1.7 pad_maximum_fusion.2
  15.8 2.0 %slice.120 = bf16[2,30,45,192]{3,2,1,0:T(8,128)(2,1)} slice(bf16[2,36,48,192]{3,2,1,0:T(8,128)(2,1)S(1)} %copy-done.8), slice={[0:2], [6:36], [3:48], [0:192]} | slice | bytes 2073600 | tf_op jit(solution)/shard_map/slice | solution.py:575
  19.3 1.1 copy.89.refs_3_
  20.5 1.2 collective-permute-start.4
  21.7 8.0 %collective-permute-done.4 = bf16[6,49]{1,0:T(8,128)(2,1)S(1)} collective-permute-done((bf16[6,49]{1,0:T(8,128)(2,1)S(1)}, bf16[6,49]{1,0:T(8,128)(2,1)S(1)}, u32[]{:S(2)}, u32[]{:S(2)}) %collective-permute-start.4) | collective-permute-done | bytes 620 | tf_op jit(solution)/shard_map/ppermute | solution.py:39
  30.7 1.1 broadcast_in_dim.31
  31.8 1.6 reshape.125.refs_11_
  34.0 1.5 slice_bitcast_fusion
  37.0 2.2 %copy.106 = bf16[2,3,12,48,192]{4,2,0,3,1:T(8,128)(2,1)} copy(bf16[2,3,12,48,192]{4,3,2,1,0:T(8,128)(2,1)S(1)} %bitcast.75) | data formatting | bytes 2654208 | tf_op jit(solution)/shard_map/reshape | solution.py:579
  39.2 4.1 %reshape.118.refs_0_ = bf16[24,144,192]{2,1,0:T(8,128)(2,1)} reshape(bf16[3,48,2,12,192]{4,3,2,1,0:T(8,128)(2,1)} %bitcast.68) | data formatting | bytes 2654208 | tf_op jit(solution)/shard_map/reshape | solution.py:581
  43.9 2.2 %copy.105 = bf16[2,3,12,48,192]{4,2,0,3,1:T(8,128)(2,1)} copy(bf16[2,3,12,48,192]{4,3,2,1,0:T(8,128)(2,1)S(1)} %bitcast.76) | data formatting | bytes 2654208 | tf_op jit(solution)/shard_map/reshape | solution.py:579
  46.0 4.2 %reshape.120.refs_1_ = bf16[24,144,192]{2,1,0:T(8,128)(2,1)} reshape(bf16[3,48,2,12,192]{4,3,2,1,0:T(8,128)(2,1)} %bitcast.69) | data formatting | bytes 2654208 | tf_op jit(solution)/shard_map/reshape | solution.py:581
  50.2 61.3 %shard_map.178 = (bf16[24,144,192]{2,1,0:T(8,128)(2,1)S(1)}, f32[6,192,128]{2,1,0:T(8,128)S(1)}, f32[24,128]{1,0:T(8,128)S(1)}, f32[13,72,128]{2,1,0:T(8,128)S(1)}) custom-call(bf16[24,144,192]{2,1,0:T(8,128)(2,1)} %reshape.118.refs_0_, bf16[24,144,192]{2,1,0:T(8,128)(2,1)} %reshape.120.refs_1_, f32[3,144,8]{2,1,0:T(8,128)S(1)} %copy.88.refs_2_, ...), custom_call_target="tpu_custom_call" | custom-call | tf_op jit(solution)/shard_map/pallas_call | solution.py:244
  111.5 27.9 %shard_map.179 = (f32[1536,128]{1,0:T(8,128)S(1)}, f32[24,128]{1,0:T(8,128)S(1)}, f32[1024,128]{1,0:T(8,128)S(1)}, f32[8,128]{1,0:T(8,128)S(1)}) custom-call(f32[1152,128]{1,0:T(8,128)S(1)} %bitcast.63, f32[24,128]{1,0:T(8,128)S(1)} %get-tuple-element.19.refs_1_, f32[936,128]{1,0:T(8,128)S(1)} %bitcast.64), custom_call_target="tpu_custom_call" | custom-call | tf_op jit(solution)/shard_map/pallas_call | solution.py:468
  141.5 2.1 %reshape.126 = bf16[3,48,2,12,192]{4,3,2,1,0:T(8,128)(2,1)} reshape(bf16[24,144,192]{2,1,0:T(8,128)(2,1)S(1)} %get-tuple-element.17) | data formatting | bytes 2654208 | tf_op jit(solution)/shard_map/reshape | solution.py:611
  143.6 2.7 %copy.90 = bf16[2,3,12,48,192]{4,3,2,1,0:T(8,128)(2,1)S(1)} copy(bf16[2,3,12,48,192]{4,2,0,3,1:T(8,128)(2,1)} %bitcast.70) | data formatting | bytes 2654208 | tf_op jit(solution)/shard_map/transpose | solution.py:611
  158.4 2.3 %collective-permute-start.5 = (bf16[2,6,3,192]{3,2,1,0:T(4,128)(2,1)S(1)}, bf16[2,6,3,192]{3,2,1,0:T(4,128)(2,1)S(1)}, u32[]{:S(2)}, u32[]{:S(2)}) collective-permute-start(bf16[2,6,3,192]{3,2,1,0:T(4,128)(2,1)S(1)} %slice.174), channel_id=1, source_target_pairs={{0,9},{1,10},{2,11},{3,12},{4,13},{5,14},{6,15},{7,8},{8,17},{9,18... | collective-permute-start | bytes 41480 | tf_op jit(solution)/shard_map/ppermute | solution.py:46
  160.7 1.3 collective-permute-start.6
  162.6 11.7 %shard_map.180 = f32[3,11,3456]{2,1,0:T(8,128)S(1)} custom-call(f32[1024,128]{1,0:T(8,128)S(1)} %get-tuple-element.23.refs_0_, f32[8,128]{1,0:T(8,128)S(1)} %get-tuple-element.24.refs_1_), custom_call_target="tpu_custom_call" | custom-call | tf_op jit(solution)/shard_map/pallas_call | solution.py:527
  174.2 1.1 copy.92
  175.3 2.1 %add_convert_fusion = bf16[2,36,48,192]{3,2,1,0:T(8,128)(2,1)} fusion(bf16[2,36,48,192]{3,2,1,0:T(8,128)(2,1)S(1)} %copy-done.4, bf16[2,30,45,192]{3,2,1,0:T(8,128)(2,1)S(1)} %slice.177, bf16[2,30,3,192]{3,2,1,0:T(4,128)(2,1)S(1)} %collective-permute-done.7, bf16[2,6,45,192]{3,2,1,0:T(8,128)(2,1)S(1)} %collective-permute-done.6, ...), kind=kLoop, calls=%fused_computation | loop fusion | flops 7299072 | bytes 3981312 | tf_op jit(solution)/shard_map/convert_element_type | solution.py:619
  (107 shorter events, 19.5 us)
Async XLA Ops:
  0.6 12.4 %copy-start.3 = (bf16[2,36,48,192]{3,2,1,0:T(8,128)(2,1)S(1)}, bf16[2,36,48,192]{3,2,1,0:T(8,128)(2,1)}, u32[]{:S(2)}) copy-start(bf16[2,36,48,192]{3,2,1,0:T(8,128)(2,1)} %param.12) | copy-start | bytes 3981316
  1.5 18.9 %collective-permute-start.3 = (bf16[36,3]{1,0:T(8,128)(2,1)S(1)}, bf16[36,3]{1,0:T(8,128)(2,1)S(1)}, u32[]{:S(2)}, u32[]{:S(2)}) collective-permute-start(bf16[36,3]{1,0:T(8,128)(2,1)S(1)} %bitcast.84), channel_id=1, source_target_pairs={{0,7},{1,0},{2,1},{3,2},{4,3},{5,4},{6,5},{7,6},{8,15},{9,8},{10,9... | collective-permute-start | bytes 656 | tf_op jit(solution)/shard_map/ppermute | solution.py:39
  3.9 29.6 %collective-permute-start.2 = (bf16[2,2,6,3,192]{4,1,3,2,0:T(2,128)(2,1)S(1)}, bf16[2,2,6,3,192]{4,1,3,2,0:T(2,128)(2,1)S(1)}, u32[]{:S(2)}, u32[]{:S(2)}) collective-permute-start(bf16[2,2,6,3,192]{4,1,3,2,0:T(2,128)(2,1)S(1)} %fusion), channel_id=1, source_target_pairs={{0,31},{1,24},{2,25},{3,26},{4,27},{5,28},{6,29},{7,30},{8,7},{9,0... | collective-permute-start | bytes 82952 | tf_op jit(solution)/shard_map/ppermute | solution.py:46
  11.5 4.2 %copy-start.12 = (s32[36]{0:T(128)S(1)}, s32[36]{0:T(128)}, u32[]{:S(2)}) copy-start(s32[36]{0:T(128)} %param.14) | copy-start | bytes 436
  11.5 4.4 %copy-start.8 = (bf16[2,36,48,192]{3,2,1,0:T(8,128)(2,1)S(1)}, bf16[2,36,48,192]{3,2,1,0:T(8,128)(2,1)}, u32[]{:S(2)}) copy-start(bf16[2,36,48,192]{3,2,1,0:T(8,128)(2,1)} %param.11) | copy-start | bytes 3981316
  11.5 22.1 %collective-permute-start = (bf16[2,2,36,3,192]{4,1,3,2,0:T(2,128)(2,1)}, bf16[2,2,36,3,192]{4,1,3,2,0:T(2,128)(2,1)S(1)}, u32[]{:S(2)}, u32[]{:S(2)}) collective-permute-start(bf16[2,2,36,3,192]{4,1,3,2,0:T(2,128)(2,1)} %pad_maximum_fusion.5), channel_id=1, source_target_pairs={{0,7},{1,0},{2,1},{3,2},{4,3},{5,4},{6,5},{7,6},{8,15},{9,8},{10,9... | collective-permute-start | bytes 497672 | tf_op jit(solution)/shard_map/ppermute | solution.py:39
  15.4 18.6 %collective-permute-start.1 = (bf16[2,2,6,45,192]{4,1,3,2,0:T(2,128)(2,1)}, bf16[2,2,6,45,192]{4,1,3,2,0:T(2,128)(2,1)}, u32[]{:S(2)}, u32[]{:S(2)}) collective-permute-start(bf16[2,2,6,45,192]{4,1,3,2,0:T(2,128)(2,1)} %pad_maximum_fusion.2), channel_id=1, source_target_pairs={{0,24},{8,0},{16,8},{24,16},{1,25},{9,1},{17,9},{25,17},{2,26},{10... | collective-permute-start | bytes 1244168 | tf_op jit(solution)/shard_map/ppermute | solution.py:39
  17.8 1.0 copy-start.10
  17.8 1.0 copy-start.11
  17.8 1.2 copy-start.9
  17.8 1.3 copy-start
  20.5 9.2 %collective-permute-start.4 = (bf16[6,49]{1,0:T(8,128)(2,1)S(1)}, bf16[6,49]{1,0:T(8,128)(2,1)S(1)}, u32[]{:S(2)}, u32[]{:S(2)}) collective-permute-start(bf16[6,49]{1,0:T(8,128)(2,1)S(1)} %fusion.2), channel_id=1, source_target_pairs={{0,24},{8,0},{16,8},{24,16},{1,25},{9,1},{17,9},{25,17},{2,26},{10... | collective-permute-start | bytes 1772 | tf_op jit(solution)/shard_map/ppermute | solution.py:39
  34.0 2.5 %copy-start.7 = (bf16[2,30,45,192]{3,2,1,0:T(8,128)(2,1)S(1)}, bf16[2,30,45,192]{3,2,1,0:T(8,128)(2,1)}, u32[]{:S(2)}) copy-start(bf16[2,30,45,192]{3,2,1,0:T(8,128)(2,1)} %slice.120) | copy-start | bytes 3110404
  46.0 4.2 %copy-start.1 = (f32[192]{0:T(256)S(1)}, f32[192]{0:T(256)}, u32[]{:S(2)}) copy-start(f32[192]{0:T(256)} %param.16) | copy-start | bytes 2308
  46.0 4.2 %copy-start.2 = (f32[192]{0:T(256)S(1)}, f32[192]{0:T(256)}, u32[]{:S(2)}) copy-start(f32[192]{0:T(256)} %param.17) | copy-start | bytes 2308
  140.0 3.6 %copy-start.5 = (f32[24,8,6,128]{3,1,2,0:T(8,128)}, f32[24,8,6,128]{3,1,2,0:T(8,128)S(1)}, u32[]{:S(2)}) copy-start(f32[24,8,6,128]{3,1,2,0:T(8,128)S(1)} %copy.107) | copy-start | bytes 1769476
  143.6 13.2 %copy-start.6 = (f32[24,8,6,128]{3,1,2,0:T(8,128)S(1)}, f32[24,8,6,128]{3,1,2,0:T(8,128)}, u32[]{:S(2)}) copy-start(f32[24,8,6,128]{3,1,2,0:T(8,128)} %copy-done.5) | copy-start | bytes 1769476
  158.4 16.9 %collective-permute-start.5 = (bf16[2,6,3,192]{3,2,1,0:T(4,128)(2,1)S(1)}, bf16[2,6,3,192]{3,2,1,0:T(4,128)(2,1)S(1)}, u32[]{:S(2)}, u32[]{:S(2)}) collective-permute-start(bf16[2,6,3,192]{3,2,1,0:T(4,128)(2,1)S(1)} %slice.174), channel_id=1, source_target_pairs={{0,9},{1,10},{2,11},{3,12},{4,13},{5,14},{6,15},{7,8},{8,17},{9,18... | collective-permute-start | bytes 41480 | tf_op jit(solution)/shard_map/ppermute | solution.py:46
  160.7 14.6 %collective-permute-start.7 = (bf16[2,30,3,192]{3,2,1,0:T(4,128)(2,1)S(1)}, bf16[2,30,3,192]{3,2,1,0:T(4,128)(2,1)S(1)}, u32[]{:S(2)}, u32[]{:S(2)}) collective-permute-start(bf16[2,30,3,192]{3,2,1,0:T(4,128)(2,1)S(1)} %slice.176), channel_id=1, source_target_pairs={{0,1},{1,2},{2,3},{3,4},{4,5},{5,6},{6,7},{7,0},{8,9},{9,10},{10,1... | collective-permute-start | bytes 207368 | tf_op jit(solution)/shard_map/ppermute | solution.py:39
  160.7 14.6 %collective-permute-start.6 = (bf16[2,6,45,192]{3,2,1,0:T(8,128)(2,1)S(1)}, bf16[2,6,45,192]{3,2,1,0:T(8,128)(2,1)S(1)}, u32[]{:S(2)}, u32[]{:S(2)}) collective-permute-start(bf16[2,6,45,192]{3,2,1,0:T(8,128)(2,1)S(1)} %slice.175), channel_id=1, source_target_pairs={{0,8},{8,16},{16,24},{24,0},{1,9},{9,17},{17,25},{25,1},{2,10},{10... | collective-permute-start | bytes 622088 | tf_op jit(solution)/shard_map/ppermute | solution.py:39
  162.6 12.7 %copy-start.4 = (bf16[2,36,48,192]{3,2,1,0:T(8,128)(2,1)S(1)}, bf16[2,36,48,192]{3,2,1,0:T(8,128)(2,1)}, u32[]{:S(2)}) copy-start(bf16[2,36,48,192]{3,2,1,0:T(8,128)(2,1)} %param.12) | copy-start | bytes 3981316

commit v3 on v2

--- a/solution.py
+++ b/solution.py
@@ -72,7 +72,7 @@
     q_row = place // WLAT % WLAT
     k_row = place % WLAT
     keep = (row == q_level * WLAT + q_row).astype(F32)
-    pick = (row == k_level * WLAT + k_row).astype(F32)
+    pick = (row == k_level * WLAT + k_row).astype(F32).astype(BF16)
     return keep, pick
 
 
@@ -121,17 +121,13 @@
         keep, pick = table_masks()
         for h in range(HEADS):
             own = table_ref[0, :, h * HB : (h + 1) * HB]
-            spread = (own[:, None, :] * keep[None]).reshape(TL, HB)
-            fold_s[:, h * TL : (h + 1) * TL] = (
-                lax.dot_general(
-                    pick,
-                    spread,
-                    (((1,), (1,)), ((), ())),
-                    precision=lax.Precision.HIGHEST,
-                    preferred_element_type=F32,
-                )
-                + gate_ref[0]
-            )
+            spread = gate_ref[0]
+            for _ in range(3):
+                part = own.astype(BF16).astype(F32)
+                own = own - part
+                placed = (part[:, None, :] * keep[None]).reshape(TL, HB).astype(BF16)
+                spread = spread + dot_nt(pick, placed)
+            fold_s[:, h * TL : (h + 1) * TL] = spread
         for h in range(HEADS):
             for j in range(WLON):
                 start = h * TL + (WLON - 1 - j) * COL
@@ -507,15 +503,9 @@
             start = t * bands * COL + band * COL
             fold_s[:, t * 128 : (t + 1) * 128] = table_ref[start : start + COL]
         for h in range(HEADS):
-            part = lax.dot_general(
-                fold_s[:, h * TL : (h + 1) * TL].T * factor,
-                pick,
-                (((1,), (0,)), ((), ())),
-                precision=lax.Precision.HIGHEST,
-                preferred_element_type=F32,
-            )
+            part = dot(fold_s[:, h * TL : (h + 1) * TL].T.astype(BF16), pick)
             part = part.reshape(DL, COL, HB) * keep[None]
-            out_ref[band, :, h * HB : (h + 1) * HB] = jnp.sum(part, axis=1)
+            out_ref[band, :, h * HB : (h + 1) * HB] = jnp.sum(part, axis=1) * factor
 
 
 def collapse(bands, count, table, squares):
@@ -561,15 +551,16 @@
     lon_piece = jnp.stack([states[:, :, :S_LON], cotangent[:, :, :S_LON]])
     lat_piece = jnp.stack([states[:, :S_LAT, S_LON:], cotangent[:, :S_LAT, S_LON:]])
     land_low = land_mask.astype(BF16)
-    pole_low = pole_mask.astype(BF16)
     lon_rim = moved(lon_piece, "lon", sizes, -1)
     lat_rim = moved(lat_piece, "lat", sizes, -1)
     corner = moved(lon_piece[:, :, :S_LAT], both, sizes, -1)
-    land_ahead = jnp.concatenate([land_low[:, S_LON:], moved(land_low[:, :S_LON], "lon", sizes, -1)], axis=1)
-    small = jnp.concatenate([land_ahead[:S_LAT], pole_low[:S_LAT, None]], axis=1)
-    small_rim = moved(small, "lat", sizes, -1)
-    rolled_land = jnp.concatenate([land_ahead[S_LAT:], small_rim[:, :cols]], axis=0).astype(F32)
-    rolled_pole = jnp.concatenate([pole_low[S_LAT:], small_rim[:, cols]], axis=0).astype(F32)
+    land_lon = moved(land_low[:, :S_LON], "lon", sizes, -1)
+    land_lat = moved(land_low[:S_LAT, S_LON:], "lat", sizes, -1)
+    land_corner = moved(land_low[:S_LAT, :S_LON], both, sizes, -1)
+    land_top = jnp.concatenate([land_low[S_LAT:, S_LON:], land_lon[S_LAT:]], axis=1)
+    land_rest = jnp.concatenate([land_lat, land_corner], axis=1)
+    rolled_land = jnp.concatenate([land_top, land_rest], axis=0).astype(F32)
+    rolled_pole = jnp.concatenate([pole_mask[S_LAT:], jnp.ones((S_LAT,), jnp.int32)])
 
     def windowed(own, at):
         top = jnp.concatenate([own[:, S_LAT:, S_LON:], lon_rim[at][:, S_LAT:]], axis=2)
@@ -588,7 +579,7 @@
     total_rows = rows * sizes["lat"]
     row_ids = lax.axis_index("lat") * rows + jnp.arange(rows, dtype=jnp.int32)
     part = (row_ids >= total_rows - S_LAT).reshape(bands, WLAT)
-    valid = (rolled_pole > 0.5).reshape(bands, WLAT)
+    valid = (rolled_pole > 0).reshape(bands, WLAT)
     allowed = (part[:, :, None] == part[:, None, :]) & valid[:, :, None]
     gate = jnp.where(allowed[:, None, :, None, None, :], 0.0, FAR)
     gate = jnp.broadcast_to(gate, (bands, PL, WLAT, DL, PL, WLAT)).reshape(bands, COL, TL)

time: 179 us -> 176 us (0.983)
  Pallas kernels: 101 us -> 88.7 us
  waiting for transfers between devices: 7.98 us -> 16.9 us
    pallas_call x1, Pallas kernels: 11.7 us -> 2.75 us  [collapse(): pl.pallas_call(body, in_specs=[vmem] * 2, out_specs=vmem, out_shape=jax.S...]
    ppermute x6, waiting for transfers between devices: 7.98 us -> 16.9 us  [moved(): lax.ppermute(array, axes, [(i, (i + by) % size) for i in range(size)])]
    pallas_call x1, Pallas kernels: 61.3 us -> 56.3 us  [attend(): pl.pallas_call(body, grid=(bands, steps), in_specs=[win_spec, win_spec, p...]
    ppermute x2 -> x3, starting transfers between devices: 8.87 us -> 5.16 us  [moved(): return lax.ppermute(array, axes, pairs)]
    ppermute x6, starting transfers between devices: 3.26 us -> 6.22 us  [moved(): lax.ppermute(array, axes, [(i, (i + by) % size) for i in range(size)])]
    pallas_call x1, Pallas kernels: 27.9 us -> 29.7 us  [exchange(): pl.pallas_call(body, in_specs=[vmem] * 3, out_specs=[vmem] * 4, out_shape...]
  transfers between devices with their start and end apart: 8 -> 9, of which waited for: 1 -> 2; matrix products, arithmetic and copies ran while one was open for 10% -> 10% of each run, Pallas kernels for 7% -> 2%
where the time goes in v3:
time: 176 us; the launch traced here: 174 us
  Pallas kernels  88.7 us (50%)
  local copies, waits for them, and re-layouts  34.5 us (20%)
  other arithmetic  16.9 us (10%)
  waiting for transfers between devices  16.9 us (10%)
  starting transfers between devices  11.4 us (6%)
  between operations  5.93 us (3%)
    pallas_call x1, Pallas kernels, attend(): pl.pallas_call(body, grid=(bands, steps), in_specs=[win_spec, win_spec, p...  56.3 us
    pallas_call x1, Pallas kernels, exchange(): pl.pallas_call(body, in_specs=[vmem] * 3, out_specs=[vmem] * 4, out_shape...  29.7 us
    ppermute x6, waiting for transfers between devices, moved(): lax.ppermute(array, axes, [(i, (i + by) % size) for i in range(size)])  16.9 us
    reshape x2, local copies, waits for them, and re-layouts, windowed(): return grid.reshape(PL, bands, WLAT, cols, C).transpose(1, 3, 0, 2, 4).re...  8.32 us
    ppermute x6, starting transfers between devices, moved(): lax.ppermute(array, axes, [(i, (i + by) % size) for i in range(size)])  6.22 us
    ppermute x3, starting transfers between devices, moved(): return lax.ppermute(array, axes, pairs)  5.16 us
    reduce_sum x7, other arithmetic, normalize_rms(): rms_value = jnp.sqrt(jnp.mean(gradient * gradient) + RMS_EPSILON)  4.45 us
    mul x7, other arithmetic, normalize_rms(): return gradient * (TARGET_RMS / rms_value)  4.41 us
  transfers between devices with their start and end apart: 9, of which 2 were waited for; matrix products, arithmetic and copies ran while one was open for 10% of the time, Pallas kernels for 2%

profile of v3, /device:TPU:1, one launch (start us, length us, event | category | flops | bytes accessed | tf_op | source)
XLA Modules:
  0.0 174.4 jit_solution(16285812087664585837)
XLA Ops:
  1.6 3.0 %collective-permute-start.4 = (bf16[6,45]{1,0:T(8,128)(2,1)S(1)}, bf16[6,45]{1,0:T(8,128)(2,1)S(1)}, u32[]{:S(2)}, u32[]{:S(2)}) collective-permute-start(bf16[6,45]{1,0:T(8,128)(2,1)S(1)} %slice.165), channel_id=1, source_target_pairs={{0,24},{8,0},{16,8},{24,16},{1,25},{9,1},{17,9},{25,17},{2,26},{10... | collective-permute-start | bytes 1628 | tf_op jit(solution)/shard_map/ppermute | solution.py:39
  4.6 1.1 collective-permute-start.5
  5.7 2.6 %collective-permute-start.3 = (bf16[36,3]{1,0:T(8,128)(2,1)S(1)}, bf16[36,3]{1,0:T(8,128)(2,1)S(1)}, u32[]{:S(2)}, u32[]{:S(2)}) collective-permute-start(bf16[36,3]{1,0:T(8,128)(2,1)S(1)} %bitcast.81), channel_id=1, source_target_pairs={{0,7},{1,0},{2,1},{3,2},{4,3},{5,4},{6,5},{7,6},{8,15},{9,8},{10,9... | collective-permute-start | bytes 656 | tf_op jit(solution)/shard_map/ppermute | solution.py:39
  10.6 2.2 %collective-permute-start.2 = (bf16[2,2,6,3,192]{4,1,3,2,0:T(2,128)(2,1)S(1)}, bf16[2,2,6,3,192]{4,1,3,2,0:T(2,128)(2,1)S(1)}, u32[]{:S(2)}, u32[]{:S(2)}) collective-permute-start(bf16[2,2,6,3,192]{4,1,3,2,0:T(2,128)(2,1)S(1)} %fusion), channel_id=1, source_target_pairs={{0,31},{1,24},{2,25},{3,26},{4,27},{5,28},{6,29},{7,30},{8,7},{9,0... | collective-permute-start | bytes 82952 | tf_op jit(solution)/shard_map/ppermute | solution.py:46
  15.0 3.3 %slice.114 = bf16[2,30,45,192]{3,2,1,0:T(8,128)(2,1)} slice(bf16[2,36,48,192]{3,2,1,0:T(8,128)(2,1)} %param.11), slice={[0:2], [6:36], [3:48], [0:192]} | slice | bytes 2073600 | tf_op jit(solution)/shard_map/slice | solution.py:566
  20.4 1.7 pad_maximum_fusion.2
  22.2 1.1 copy.84.refs_3_
  23.4 1.1 broadcast_in_dim.27
  24.5 1.6 reshape.117.refs_11_
  27.6 12.4 %collective-permute-done.1 = bf16[2,2,6,45,192]{4,1,3,2,0:T(2,128)(2,1)} collective-permute-done((bf16[2,2,6,45,192]{4,1,3,2,0:T(2,128)(2,1)}, bf16[2,2,6,45,192]{4,1,3,2,0:T(2,128)(2,1)}, u32[]{:S(2)}, u32[]{:S(2)}) %collective-permute-start.1) | collective-permute-done | bytes 414752 | tf_op jit(solution)/shard_map/ppermute | solution.py:39
  40.0 1.4 slice_bitcast_fusion
  42.9 2.2 %copy.101 = bf16[2,3,12,48,192]{4,2,0,3,1:T(8,128)(2,1)} copy(bf16[2,3,12,48,192]{4,3,2,1,0:T(8,128)(2,1)S(1)} %bitcast.72) | data formatting | bytes 2654208 | tf_op jit(solution)/shard_map/reshape | solution.py:570
  45.1 4.1 %reshape.110.refs_0_ = bf16[24,144,192]{2,1,0:T(8,128)(2,1)} reshape(bf16[3,48,2,12,192]{4,3,2,1,0:T(8,128)(2,1)} %bitcast.65) | data formatting | bytes 2654208 | tf_op jit(solution)/shard_map/reshape | solution.py:572
  49.8 2.2 %copy.100 = bf16[2,3,12,48,192]{4,2,0,3,1:T(8,128)(2,1)} copy(bf16[2,3,12,48,192]{4,3,2,1,0:T(8,128)(2,1)S(1)} %bitcast.73) | data formatting | bytes 2654208 | tf_op jit(solution)/shard_map/reshape | solution.py:570
  52.0 4.2 %reshape.112.refs_1_ = bf16[24,144,192]{2,1,0:T(8,128)(2,1)} reshape(bf16[3,48,2,12,192]{4,3,2,1,0:T(8,128)(2,1)} %bitcast.66) | data formatting | bytes 2654208 | tf_op jit(solution)/shard_map/reshape | solution.py:572
  56.1 56.3 %shard_map.178 = (bf16[24,144,192]{2,1,0:T(8,128)(2,1)S(1)}, f32[6,192,128]{2,1,0:T(8,128)S(1)}, f32[24,128]{1,0:T(8,128)S(1)}, f32[13,72,128]{2,1,0:T(8,128)S(1)}) custom-call(bf16[24,144,192]{2,1,0:T(8,128)(2,1)} %reshape.110.refs_0_, bf16[24,144,192]{2,1,0:T(8,128)(2,1)} %reshape.112.refs_1_, f32[3,144,8]{2,1,0:T(8,128)S(1)} %copy.83.refs_2_, ...), custom_call_target="tpu_custom_call" | custom-call | tf_op jit(solution)/shard_map/pallas_call | solution.py:240
  112.4 29.7 %shard_map.179 = (f32[1536,128]{1,0:T(8,128)S(1)}, f32[24,128]{1,0:T(8,128)S(1)}, f32[1024,128]{1,0:T(8,128)S(1)}, f32[8,128]{1,0:T(8,128)S(1)}) custom-call(f32[1152,128]{1,0:T(8,128)S(1)} %bitcast.60, f32[24,128]{1,0:T(8,128)S(1)} %get-tuple-element.19.refs_1_, f32[936,128]{1,0:T(8,128)S(1)} %bitcast.61), custom_call_target="tpu_custom_call" | custom-call | tf_op jit(solution)/shard_map/pallas_call | solution.py:464
  144.2 2.1 %reshape.118 = bf16[3,48,2,12,192]{4,3,2,1,0:T(8,128)(2,1)} reshape(bf16[24,144,192]{2,1,0:T(8,128)(2,1)S(1)} %get-tuple-element.17) | data formatting | bytes 2654208 | tf_op jit(solution)/shard_map/reshape | solution.py:602
  146.3 2.7 %copy.85 = bf16[2,3,12,48,192]{4,3,2,1,0:T(8,128)(2,1)S(1)} copy(bf16[2,3,12,48,192]{4,2,0,3,1:T(8,128)(2,1)} %bitcast.67) | data formatting | bytes 2654208 | tf_op jit(solution)/shard_map/transpose | solution.py:602
  161.1 1.8 %collective-permute-start.6 = (bf16[2,6,3,192]{3,2,1,0:T(4,128)(2,1)S(1)}, bf16[2,6,3,192]{3,2,1,0:T(4,128)(2,1)S(1)}, u32[]{:S(2)}, u32[]{:S(2)}) collective-permute-start(bf16[2,6,3,192]{3,2,1,0:T(4,128)(2,1)S(1)} %slice.167), channel_id=1, source_target_pairs={{0,9},{1,10},{2,11},{3,12},{4,13},{5,14},{6,15},{7,8},{8,17},{9,18... | collective-permute-start | bytes 41480 | tf_op jit(solution)/shard_map/ppermute | solution.py:46
  163.9 2.7 %shard_map.180 = f32[3,11,3456]{2,1,0:T(8,128)S(1)} custom-call(f32[1024,128]{1,0:T(8,128)S(1)} %get-tuple-element.23.refs_0_, f32[8,128]{1,0:T(8,128)S(1)} %get-tuple-element.24.refs_1_), custom_call_target="tpu_custom_call" | custom-call | tf_op jit(solution)/shard_map/pallas_call | solution.py:517
  166.7 1.1 copy.87
  167.7 4.5 %collective-permute-done.7 = bf16[2,6,45,192]{3,2,1,0:T(8,128)(2,1)S(1)} collective-permute-done((bf16[2,6,45,192]{3,2,1,0:T(8,128)(2,1)S(1)}, bf16[2,6,45,192]{3,2,1,0:T(8,128)(2,1)S(1)}, u32[]{:S(2)}, u32[]{:S(2)}) %collective-permute-start.7) | collective-permute-done | bytes 207392 | tf_op jit(solution)/shard_map/ppermute | solution.py:39
  172.2 2.1 %add_convert_fusion = bf16[2,36,48,192]{3,2,1,0:T(8,128)(2,1)} fusion(bf16[2,36,48,192]{3,2,1,0:T(8,128)(2,1)S(1)} %copy-done.4, bf16[2,30,45,192]{3,2,1,0:T(8,128)(2,1)S(1)} %slice.170, bf16[2,30,3,192]{3,2,1,0:T(4,128)(2,1)S(1)} %collective-permute-done.8, bf16[2,6,45,192]{3,2,1,0:T(8,128)(2,1)S(1)} %collective-permute-done.7, ...), kind=kLoop, calls=%fused_computation | loop fusion | flops 7299072 | bytes 3981312 | tf_op jit(solution)/shard_map/convert_element_type | solution.py:610
  (104 shorter events, 21.0 us)
Async XLA Ops:
  0.6 14.3 %copy-start.3 = (bf16[2,36,48,192]{3,2,1,0:T(8,128)(2,1)S(1)}, bf16[2,36,48,192]{3,2,1,0:T(8,128)(2,1)}, u32[]{:S(2)}) copy-start(bf16[2,36,48,192]{3,2,1,0:T(8,128)(2,1)} %param.12) | copy-start | bytes 3981316
  1.6 24.9 %collective-permute-start.4 = (bf16[6,45]{1,0:T(8,128)(2,1)S(1)}, bf16[6,45]{1,0:T(8,128)(2,1)S(1)}, u32[]{:S(2)}, u32[]{:S(2)}) collective-permute-start(bf16[6,45]{1,0:T(8,128)(2,1)S(1)} %slice.165), channel_id=1, source_target_pairs={{0,24},{8,0},{16,8},{24,16},{1,25},{9,1},{17,9},{25,17},{2,26},{10... | collective-permute-start | bytes 1628 | tf_op jit(solution)/shard_map/ppermute | solution.py:39
  4.6 21.8 %collective-permute-start.5 = (bf16[6,3]{1,0:T(8,128)(2,1)S(1)}, bf16[6,3]{1,0:T(8,128)(2,1)S(1)}, u32[]{:S(2)}, u32[]{:S(2)}) collective-permute-start(bf16[6,3]{1,0:T(8,128)(2,1)S(1)} %slice.166), channel_id=1, source_target_pairs={{0,31},{1,24},{2,25},{3,26},{4,27},{5,28},{6,29},{7,30},{8,7},{9,0... | collective-permute-start | bytes 116 | tf_op jit(solution)/shard_map/ppermute | solution.py:46
  5.7 20.4 %collective-permute-start.3 = (bf16[36,3]{1,0:T(8,128)(2,1)S(1)}, bf16[36,3]{1,0:T(8,128)(2,1)S(1)}, u32[]{:S(2)}, u32[]{:S(2)}) collective-permute-start(bf16[36,3]{1,0:T(8,128)(2,1)S(1)} %bitcast.81), channel_id=1, source_target_pairs={{0,7},{1,0},{2,1},{3,2},{4,3},{5,4},{6,5},{7,6},{8,15},{9,8},{10,9... | collective-permute-start | bytes 656 | tf_op jit(solution)/shard_map/ppermute | solution.py:39
  10.6 16.6 %collective-permute-start.2 = (bf16[2,2,6,3,192]{4,1,3,2,0:T(2,128)(2,1)S(1)}, bf16[2,2,6,3,192]{4,1,3,2,0:T(2,128)(2,1)S(1)}, u32[]{:S(2)}, u32[]{:S(2)}) collective-permute-start(bf16[2,2,6,3,192]{4,1,3,2,0:T(2,128)(2,1)S(1)} %fusion), channel_id=1, source_target_pairs={{0,31},{1,24},{2,25},{3,26},{4,27},{5,28},{6,29},{7,30},{8,7},{9,0... | collective-permute-start | bytes 82952 | tf_op jit(solution)/shard_map/ppermute | solution.py:46
  13.8 13.4 %collective-permute-start = (bf16[2,2,36,3,192]{4,1,3,2,0:T(2,128)(2,1)}, bf16[2,2,36,3,192]{4,1,3,2,0:T(2,128)(2,1)S(1)}, u32[]{:S(2)}, u32[]{:S(2)}) collective-permute-start(bf16[2,2,36,3,192]{4,1,3,2,0:T(2,128)(2,1)} %pad_maximum_fusion.5), channel_id=1, source_target_pairs={{0,7},{1,0},{2,1},{3,2},{4,3},{5,4},{6,5},{7,6},{8,15},{9,8},{10,9... | collective-permute-start | bytes 497672 | tf_op jit(solution)/shard_map/ppermute | solution.py:39
  18.3 0.9 copy-start.11
  18.3 1.1 copy-start.9
  18.3 1.1 copy-start.10
  18.3 1.2 copy-start.8
  19.2 2.9 %copy-start = (bf16[192,576]{1,0:T(8,128)(2,1)S(1)}, bf16[192,576]{1,0:T(8,128)(2,1)}, u32[]{:S(2)}) copy-start(bf16[192,576]{1,0:T(8,128)(2,1)} %refs_6_.1) | copy-start | bytes 663556
  26.1 13.9 %collective-permute-start.1 = (bf16[2,2,6,45,192]{4,1,3,2,0:T(2,128)(2,1)}, bf16[2,2,6,45,192]{4,1,3,2,0:T(2,128)(2,1)}, u32[]{:S(2)}, u32[]{:S(2)}) collective-permute-start(bf16[2,2,6,45,192]{4,1,3,2,0:T(2,128)(2,1)} %pad_maximum_fusion.2), channel_id=1, source_target_pairs={{0,24},{8,0},{16,8},{24,16},{1,25},{9,1},{17,9},{25,17},{2,26},{10... | collective-permute-start | bytes 1244168 | tf_op jit(solution)/shard_map/ppermute | solution.py:39
  27.6 14.8 %copy-start.7 = (bf16[2,30,45,192]{3,2,1,0:T(8,128)(2,1)S(1)}, bf16[2,30,45,192]{3,2,1,0:T(8,128)(2,1)}, u32[]{:S(2)}) copy-start(bf16[2,30,45,192]{3,2,1,0:T(8,128)(2,1)} %slice.114) | copy-start | bytes 3110404
  52.0 4.2 %copy-start.1 = (f32[192]{0:T(256)S(1)}, f32[192]{0:T(256)}, u32[]{:S(2)}) copy-start(f32[192]{0:T(256)} %param.16) | copy-start | bytes 2308
  52.0 4.2 %copy-start.2 = (f32[192]{0:T(256)S(1)}, f32[192]{0:T(256)}, u32[]{:S(2)}) copy-start(f32[192]{0:T(256)} %param.17) | copy-start | bytes 2308
  142.7 3.6 %copy-start.5 = (f32[24,8,6,128]{3,1,2,0:T(8,128)}, f32[24,8,6,128]{3,1,2,0:T(8,128)S(1)}, u32[]{:S(2)}) copy-start(f32[24,8,6,128]{3,1,2,0:T(8,128)S(1)} %copy.102) | copy-start | bytes 1769476
  146.3 13.2 %copy-start.6 = (f32[24,8,6,128]{3,1,2,0:T(8,128)S(1)}, f32[24,8,6,128]{3,1,2,0:T(8,128)}, u32[]{:S(2)}) copy-start(f32[24,8,6,128]{3,1,2,0:T(8,128)} %copy-done.5) | copy-start | bytes 1769476
  161.1 6.6 %collective-permute-start.6 = (bf16[2,6,3,192]{3,2,1,0:T(4,128)(2,1)S(1)}, bf16[2,6,3,192]{3,2,1,0:T(4,128)(2,1)S(1)}, u32[]{:S(2)}, u32[]{:S(2)}) collective-permute-start(bf16[2,6,3,192]{3,2,1,0:T(4,128)(2,1)S(1)} %slice.167), channel_id=1, source_target_pairs={{0,9},{1,10},{2,11},{3,12},{4,13},{5,14},{6,15},{7,8},{8,17},{9,18... | collective-permute-start | bytes 41480 | tf_op jit(solution)/shard_map/ppermute | solution.py:46
  163.0 4.8 %collective-permute-start.8 = (bf16[2,30,3,192]{3,2,1,0:T(4,128)(2,1)S(1)}, bf16[2,30,3,192]{3,2,1,0:T(4,128)(2,1)S(1)}, u32[]{:S(2)}, u32[]{:S(2)}) collective-permute-start(bf16[2,30,3,192]{3,2,1,0:T(4,128)(2,1)S(1)} %slice.169), channel_id=1, source_target_pairs={{0,1},{1,2},{2,3},{3,4},{4,5},{5,6},{6,7},{7,0},{8,9},{9,10},{10,1... | collective-permute-start | bytes 207368 | tf_op jit(solution)/shard_map/ppermute | solution.py:39
  163.0 9.2 %collective-permute-start.7 = (bf16[2,6,45,192]{3,2,1,0:T(8,128)(2,1)S(1)}, bf16[2,6,45,192]{3,2,1,0:T(8,128)(2,1)S(1)}, u32[]{:S(2)}, u32[]{:S(2)}) collective-permute-start(bf16[2,6,45,192]{3,2,1,0:T(8,128)(2,1)S(1)} %slice.168), channel_id=1, source_target_pairs={{0,8},{8,16},{16,24},{24,0},{1,9},{9,17},{17,25},{25,1},{2,10},{10... | collective-permute-start | bytes 622088 | tf_op jit(solution)/shard_map/ppermute | solution.py:39
  163.9 8.3 %copy-start.4 = (bf16[2,36,48,192]{3,2,1,0:T(8,128)(2,1)S(1)}, bf16[2,36,48,192]{3,2,1,0:T(8,128)(2,1)}, u32[]{:S(2)}) copy-start(bf16[2,36,48,192]{3,2,1,0:T(8,128)(2,1)} %param.12) | copy-start | bytes 3981316
